TPU v7x, 512 devices: a whole 4x4x16 slice. The times are simulated.
512 devices in a mesh: span: 32 (over z, core), local: 16 (over y, x).
Axes of the slice: x: 4, y: 4, z: 16, core: 2. Of those that a mesh axis runs over, the one named last changes fastest.
Arguments:
- queries: bfloat16 [65536, 2560], P(('span', 'local')), may hold values from -8 to 8
- keys: bfloat16 [32768, 512], P(('span', 'local')), may hold values from -8 to 8
- values: bfloat16 [32768, 512], P(('span', 'local')), may hold values from -6 to 6
- far_blocks: int32 [512, 4, 4], P(('span', 'local')), may hold values from 0 to 255, as said below
- far_live_length: int32 [512, 4], P(('span', 'local')), may hold values from 3 to 4
Outputs:
- attended: bfloat16 [65536, 2560], P(('span', 'local'))
Inputs may be any that keep to these rules, and one draw needn't show every extreme that they name: `far_blocks`: entry c names key block c. Every an entry of value names a block outside the span group of its query block, and the entries of one list are distinct. Among the live entries (list position below far_live_length) of the lists of one device's 1 query block, at most 2 name blocks of any one span group, and in every draw some span group is named exactly 2 times by each device's lists. `far_live_length`: list entries at positions from the count on are ignored.
All inputs are finite; a program needn't handle non-finite values.
Results may differ from a plain program's by a relative error of at most 0.0047.
Values may be sent and summed in bfloat16 or wider, within the bound.
No kernel may reach another device: no remote copies, remote signals or barrier semaphores. Data moves between devices by JAX's collectives and lax.ppermute only.
A program may use at most 64 MiB of HBM per device.

v0:
```python
import math

import jax
import jax.numpy as jnp
from jax import lax
from jax.sharding import PartitionSpec as P

QUERY_HEADS = 20
KEY_HEADS = 4
HEAD_WIDTH = 128
BLOCK_WIDTH = 128


def route_lists(blocks, counts, span_block_tiles, span_block_count, list_capacity):
    heads_kv = blocks.shape[1]
    flat = blocks.reshape(-1)
    slot_pos = lax.broadcasted_iota(jnp.int32, blocks.shape, 2)
    head_pos = lax.broadcasted_iota(jnp.int32, blocks.shape, 1).reshape(-1)
    live_entries = (slot_pos < counts[:, :, None]).reshape(-1)
    target = flat // span_block_tiles
    spans = jnp.arange(span_block_count, dtype=jnp.int32)
    member = jnp.logical_and(target[:, None] == spans[None, :], live_entries[:, None]).astype(
        jnp.int32
    )
    place = jnp.sum((jnp.cumsum(member, axis=0) - member) * member, axis=1)
    code = flat % span_block_tiles * heads_kv + head_pos
    slots = jnp.arange(list_capacity, dtype=jnp.int32)
    hit = jnp.logical_and(
        member[:, :, None] > 0, place[:, None, None] == slots[None, None, :]
    ).astype(jnp.int32)
    requests = jnp.sum(hit * (code + 1)[:, None, None], axis=0) - 1
    source_device = jnp.where(live_entries, target * list_capacity + place, 0)
    return (requests, source_device, live_entries)


def serve_blocks(table_k, table_v, requests):
    index = jnp.maximum(requests, 0)
    present = (requests >= 0)[..., None, None]
    got_k = jnp.where(present, jnp.take(table_k, index, axis=0), jnp.zeros((), jnp.bfloat16))
    got_v = jnp.where(present, jnp.take(table_v, index, axis=0), jnp.zeros((), jnp.bfloat16))
    return (got_k, got_v)


def attend_all(queries, near_key_rows, near_value_rows, far_key_rows, far_value_rows, live_entries):
    query_block_rows = queries.shape[0] // BLOCK_WIDTH
    head_group = QUERY_HEADS // KEY_HEADS
    span_key_rows = near_key_rows.shape[0]
    scale = 1.0 / math.sqrt(HEAD_WIDTH)
    query_block_tiles = queries.reshape(
        query_block_rows, BLOCK_WIDTH, KEY_HEADS, head_group, HEAD_WIDTH
    )
    near_key_rows3 = near_key_rows.reshape(span_key_rows, KEY_HEADS, HEAD_WIDTH)
    near_value_rows3 = near_value_rows.reshape(span_key_rows, KEY_HEADS, HEAD_WIDTH)
    results = []
    for head_slot in range(KEY_HEADS):
        query_h = query_block_tiles[:, :, head_slot]
        near_s = (
            jnp.einsum(
                "bqgd,kd->bgqk",
                query_h,
                near_key_rows3[:, head_slot],
                preferred_element_type=jnp.float32,
            )
            * scale
        )
        far_s = (
            jnp.einsum(
                "bqgd,bfkd->bgqfk",
                query_h,
                far_key_rows[:, head_slot],
                preferred_element_type=jnp.float32,
            )
            * scale
        )
        mask = live_entries[:, head_slot][:, None, None, :, None]
        far_s = jnp.where(mask, far_s, -1e30)
        top = jnp.maximum(jnp.max(near_s, axis=-1), jnp.max(far_s, axis=(-2, -1)))
        near_w = jnp.exp(near_s - top[..., None])
        far_w = jnp.exp(far_s - top[..., None, None])
        total = jnp.sum(near_w, axis=-1) + jnp.sum(far_w, axis=(-2, -1))
        acc = jnp.einsum(
            "bgqk,kd->bgqd",
            near_w.astype(jnp.bfloat16),
            near_value_rows3[:, head_slot],
            preferred_element_type=jnp.float32,
        )
        acc = acc + jnp.einsum(
            "bgqfk,bfkd->bgqd",
            far_w.astype(jnp.bfloat16),
            far_value_rows[:, head_slot],
            preferred_element_type=jnp.float32,
        )
        results.append((acc / total[..., None]).transpose(0, 2, 1, 3))
    stacked = jnp.stack(results, axis=2)
    return stacked.reshape(queries.shape[0], QUERY_HEADS * HEAD_WIDTH).astype(jnp.bfloat16)


def local(queries, keys, values, far_blocks, far_live_length):
    span_block_count = lax.axis_size("span")
    query_block_rows = queries.shape[0] // BLOCK_WIDTH
    far_list_length = far_blocks.shape[2]
    list_capacity = max(
        2,
        (query_block_rows * KEY_HEADS * far_list_length + span_block_count - 2)
        // (span_block_count - 1),
    )
    near_key_rows, near_value_rows = (
        lax.all_gather(keys, "local", axis=0, tiled=True),
        lax.all_gather(values, "local", axis=0, tiled=True),
    )
    span_block_tiles = near_key_rows.shape[0] // BLOCK_WIDTH
    table_k = (
        near_key_rows.reshape(span_block_tiles, BLOCK_WIDTH, KEY_HEADS, HEAD_WIDTH)
        .transpose(0, 2, 1, 3)
        .reshape(span_block_tiles * KEY_HEADS, BLOCK_WIDTH, HEAD_WIDTH)
    )
    table_v = (
        near_value_rows.reshape(span_block_tiles, BLOCK_WIDTH, KEY_HEADS, HEAD_WIDTH)
        .transpose(0, 2, 1, 3)
        .reshape(span_block_tiles * KEY_HEADS, BLOCK_WIDTH, HEAD_WIDTH)
    )
    requests, source_device, live_entries = route_lists(
        far_blocks, far_live_length, span_block_tiles, span_block_count, list_capacity
    )
    got_k, got_v = serve_blocks(
        table_k, table_v, lax.all_to_all(requests, "span", split_axis=0, concat_axis=0, tiled=True)
    )
    arrived_k = lax.all_to_all(got_k, "span", split_axis=0, concat_axis=0, tiled=True)
    arrived_v = lax.all_to_all(got_v, "span", split_axis=0, concat_axis=0, tiled=True)
    flattened_keys = arrived_k.reshape(span_block_count * list_capacity, BLOCK_WIDTH, HEAD_WIDTH)
    flattened_values = arrived_v.reshape(span_block_count * list_capacity, BLOCK_WIDTH, HEAD_WIDTH)
    far_key_rows = jnp.take(flattened_keys, source_device, axis=0).reshape(
        query_block_rows, KEY_HEADS, far_list_length, BLOCK_WIDTH, HEAD_WIDTH
    )
    far_value_rows = jnp.take(flattened_values, source_device, axis=0).reshape(
        query_block_rows, KEY_HEADS, far_list_length, BLOCK_WIDTH, HEAD_WIDTH
    )
    live_far_lists = live_entries.reshape(query_block_rows, KEY_HEADS, far_list_length)
    return attend_all(
        queries, near_key_rows, near_value_rows, far_key_rows, far_value_rows, live_far_lists
    )


def solution(mesh):
    placed = (
        P(("span", "local"), None),
        P(("span", "local"), None),
        P(("span", "local"), None),
        P(("span", "local"), None, None),
        P(("span", "local"), None),
    )
    return jax.shard_map(
        local, mesh=mesh, in_specs=placed, out_specs=P(("span", "local"), None), check_vma=False
    )
```

profile of v0, /device:TPU:1, one launch (start us, length us, event | category | flops | bytes accessed | tf_op | source)
XLA Modules:
  0.0 388.5 jit_solution(15178165953212279119)
XLA Ops:
  6.5 0.7 all-gather.3.cloned.1.call-update
  7.3 0.7 all-gather.5.cloned.1.call-update
  8.0 0.7 lt.44
  9.0 0.8 reshape.525
  10.3 28.3 %all_to_all.16 = s32[32,1,2]{2,1,0:T(1,128)S(1)} all-to-all(s32[32,1,2]{2,1,0:T(1,128)S(1)} %copy.178), channel_id=1, replica_groups=mesh['span'=32,'local'=16] {'span'}, dimensions={0} | all-to-all | bytes 512 | tf_op jit(solution)/shard_map/all_to_all | solution.py:126
  39.1 33.1 %all-gather.3.cloned.1.call-done = bf16[1024,512]{1,0:T(8,128)(2,1)} async-done(((bf16[64,512]{1,0:T(8,128)(2,1)}), bf16[1024,512]{1,0:T(8,128)(2,1)}) %all-gather.3.cloned.1.call-update) | async-done | bytes 1048592 | tf_op jit(solution)/shard_map/all_gather | solution.py:108
  72.3 1.3 reshape.629
  73.9 58.8 %all-gather.5.cloned.1.call-done = bf16[1024,512]{1,0:T(8,128)(2,1)} async-done(((bf16[64,512]{1,0:T(8,128)(2,1)}), bf16[1024,512]{1,0:T(8,128)(2,1)}) %all-gather.5.cloned.1.call-update) | async-done | bytes 1048592 | tf_op jit(solution)/shard_map/all_gather | solution.py:109
  132.7 1.3 reshape.630
  134.3 2.1 gather_fusion
  136.4 2.2 gather_fusion.2
  138.6 3.6 select_select_fusion
  142.1 115.0 %all_to_all.17 = bf16[32,2,128,128]{3,2,1,0:T(8,128)(2,1)} all-to-all(bf16[32,2,128,128]{3,2,1,0:T(8,128)(2,1)S(1)} %get-tuple-element.10), channel_id=1, replica_groups=mesh['span'=32,'local'=16] {'span'}, dimensions={0} | all-to-all | bytes 4194304 | tf_op jit(solution)/shard_map/all_to_all | solution.py:128
  257.1 5.0 %all-to-all-start.2 = ((bf16[32,2,128,128]{3,2,1,0:T(8,128)(2,1)}), bf16[32,2,128,128]{3,2,1,0:T(8,128)(2,1)}, u32[]{:S(2)}, u32[]{:S(2)}) async-start(bf16[32,2,128,128]{3,2,1,0:T(8,128)(2,1)} %get-tuple-element.9), calls=%async_computation.2 | async-start | bytes 4194304 | tf_op jit(solution)/shard_map/all_to_all | solution.py:129
  263.2 2.7 copy.186
  265.8 2.0 bitcast_reduce_fusion.3
  267.9 2.1 bitcast_reduce_fusion.2
  269.9 2.0 bitcast_reduce_fusion.1
  271.9 1.5 bitcast_reduce_fusion
  273.4 3.0 gather_fusion.1
  276.5 85.5 %all-to-all-done.2 = bf16[32,2,128,128]{3,2,1,0:T(8,128)(2,1)} async-done(((bf16[32,2,128,128]{3,2,1,0:T(8,128)(2,1)}), bf16[32,2,128,128]{3,2,1,0:T(8,128)(2,1)}, u32[]{:S(2)}, u32[]{:S(2)}) %all-to-all-start.2) | async-done | bytes 2097184 | tf_op jit(solution)/shard_map/all_to_all | solution.py:129
  362.0 3.0 gather_fusion.3
  365.0 2.3 broadcast_select_fusion
  367.3 2.1 copy.192
  369.4 1.3 bitcast_reduce_fusion.7
  374.1 0.8 copy-done.2
  376.3 0.6 copy-done
  378.0 0.6 fusion.97
  378.6 0.6 fusion.94
  379.3 0.6 fusion.91
  379.9 0.6 fusion.88
  380.6 1.1 copy.206
  (75 shorter events, 8.7 us)
Async XLA Ops:
  6.5 65.8 %all-gather.3.cloned.1.call-start = ((), (), s32[]{:S(2)}) async-start(), calls=%async_computation.3 | async-start | bytes 1114112 | tf_op jit(solution)/shard_map/all_gather | solution.py:108
  7.3 125.4 %all-gather.5.cloned.1.call-start = ((), (), s32[]{:S(2)}) async-start(), calls=%async_computation.4 | async-start | bytes 1114112 | tf_op jit(solution)/shard_map/all_gather | solution.py:109
  257.1 5.0 %copy-start.8 = (bf16[128,2560]{1,0:T(8,128)(2,1)S(1)}, bf16[128,2560]{1,0:T(8,128)(2,1)}, u32[]{:S(2)}) copy-start(bf16[128,2560]{1,0:T(8,128)(2,1)} %param.9) | copy-start | bytes 1966084
  257.1 5.4 %copy-start.9 = (s32[1,4]{1,0:T(1,128)S(1)}, s32[1,4]{1,0:T(1,128)}, u32[]{:S(2)}) copy-start(s32[1,4]{1,0:T(1,128)} %param.13) | copy-start | bytes 52
  257.1 5.5 %copy-start.4 = (bf16[1024,512]{1,0:T(8,128)(2,1)S(1)}, bf16[1024,512]{1,0:T(8,128)(2,1)}, u32[]{:S(2)}) copy-start(bf16[1024,512]{1,0:T(8,128)(2,1)} %all-gather.3.cloned.1.call-done) | copy-start | bytes 3145732
  257.1 104.8 %all-to-all-start.2 = ((bf16[32,2,128,128]{3,2,1,0:T(8,128)(2,1)}), bf16[32,2,128,128]{3,2,1,0:T(8,128)(2,1)}, u32[]{:S(2)}, u32[]{:S(2)}) async-start(bf16[32,2,128,128]{3,2,1,0:T(8,128)(2,1)} %get-tuple-element.9), calls=%async_computation.2 | async-start | bytes 4194304 | tf_op jit(solution)/shard_map/all_to_all | solution.py:129
  263.1 6.8 %copy-start.3 = (bf16[1024,512]{0,1:T(8,128)(2,1)}, bf16[1024,512]{0,1:T(8,128)(2,1)S(1)}, u32[]{:S(2)}) copy-start(bf16[1024,512]{0,1:T(8,128)(2,1)S(1)} %copy.174) | copy-start | bytes 3145732
  369.4 1.5 copy-start.6
  369.4 1.9 copy-start.5
  373.1 1.7 copy-start.2
  373.7 2.1 copy-start.1
  374.9 1.9 copy-start
  376.8 1.2 copy-start.7
Sparse Core Ops, SparseCore 0:
  10.4 61.8 all-gather.2
  75.3 57.3 all-gather.4
where the time goes:
time: 389 us
  waiting for transfers between devices  179 us (46%)
  blocking collectives  143 us (37%)
  local copies, waits for them, and re-layouts  24.7 us (6%)
  matrix products  13.8 us (4%)
  between operations  13.8 us (4%)
  other arithmetic  9.08 us (2%)
  starting transfers between devices  5.03 us (1%)
    all_to_all x1, blocking collectives, local(): lax.all_to_all(got_k, 'span', split_axis=0, concat_axis=0, tiled=True)  115 us
    all_to_all x1, waiting for transfers between devices, local(): lax.all_to_all(got_v, 'span', split_axis=0, concat_axis=0, tiled=True)  85.5 us
    all_gather x1, waiting for transfers between devices, local(): lax.all_gather(values, 'local', axis=0, tiled=True)  58.8 us
    all_gather x1, waiting for transfers between devices, local(): lax.all_gather(keys, 'local', axis=0, tiled=True)  33.1 us
    all_to_all x1, blocking collectives, local(): lax.all_to_all(requests, 'span', split_axis=0, concat_axis=0, tiled=True)  28.3 us
  transfers between devices with their start and end apart: 3, of which 3 were waited for; matrix products, arithmetic and copies ran while one was open for 5% of the time, Pallas kernels for 0%

commit v1 on v0

v1 whole, which is shorter than its diff:
```python
import functools
import math

import jax
import jax.numpy as jnp
from jax import lax
from jax.experimental import pallas as pl
from jax.experimental.pallas import tpu as pltpu
from jax.sharding import Mesh, PartitionSpec as P

KEY_HEADS = 4
GROUP = 5
WIDTH = 128
BLOCK = 128
LIST = 4
Z, C, Y, X = 16, 2, 4, 4
LAYER = C * Y * X
KDEV = 64
ROWS = KDEV // LAYER
SHARE = 4
NEAR = Y * X * KDEV
LANES = KEY_HEADS * 2 * WIDTH
UNIT = LAYER * ROWS
SCALE = 1.0 / math.sqrt(WIDTH)
QROWS = GROUP * BLOCK


def stack_heads(q_ref):
    return jnp.concatenate([q_ref[:, h * WIDTH : (h + 1) * WIDTH] for h in range(GROUP)], axis=0)


def near_kernel(q_ref, k_ref, v_ref, acc_ref, stat_ref):
    q = stack_heads(q_ref)
    s = lax.dot_general(
        q, k_ref[...], (((1,), (1,)), ((), ())), preferred_element_type=jnp.float32
    ) * SCALE
    top = jnp.max(s, axis=1, keepdims=True)
    w = jnp.exp(s - top)
    total = jnp.sum(w, axis=1, keepdims=True)
    acc_ref[0] = jnp.dot(w.astype(jnp.bfloat16), v_ref[...], preferred_element_type=jnp.float32)
    lane = lax.broadcasted_iota(jnp.int32, (QROWS, WIDTH), 1)
    stat_ref[0] = jnp.where(lane == 0, top, total)


def near_attention(queries, near):
    return pl.pallas_call(
        near_kernel,
        grid=(KEY_HEADS,),
        in_specs=[
            pl.BlockSpec((BLOCK, GROUP * WIDTH), lambda e: (0, e)),
            pl.BlockSpec((NEAR, WIDTH), lambda e: (0, 2 * e)),
            pl.BlockSpec((NEAR, WIDTH), lambda e: (0, 2 * e + 1)),
        ],
        out_specs=[
            pl.BlockSpec((1, QROWS, WIDTH), lambda e: (e, 0, 0)),
            pl.BlockSpec((1, QROWS, WIDTH), lambda e: (e, 0, 0)),
        ],
        out_shape=[
            jax.ShapeDtypeStruct((KEY_HEADS, QROWS, WIDTH), jnp.float32),
            jax.ShapeDtypeStruct((KEY_HEADS, QROWS, WIDTH), jnp.float32),
        ],
        compiler_params=pltpu.CompilerParams(vmem_limit_bytes=40 * 1024 * 1024),
        cost_estimate=pl.CostEstimate(
            flops=4 * KEY_HEADS * QROWS * NEAR * WIDTH,
            bytes_accessed=8 * 1024 * 1024,
            transcendentals=KEY_HEADS * QROWS * NEAR,
        ),
        name="near",
    )(queries, near, near)


def far_kernel(live_ref, q_ref, k_ref, v_ref, acc_ref, stat_ref, out_ref):
    q = stack_heads(q_ref)
    s = lax.dot_general(
        q, k_ref[...], (((1,), (1,)), ((), ())), preferred_element_type=jnp.float32
    ) * SCALE
    column = lax.broadcasted_iota(jnp.int32, (1, LIST * BLOCK), 1)
    entry = (column % (LIST * SHARE)) // SHARE
    s = jnp.where(entry < live_ref[pl.program_id(0)], s, -1e30)
    near_top = stat_ref[0][:, 0:1]
    near_total = stat_ref[0][:, 1:2]
    top = jnp.maximum(near_top, jnp.max(s, axis=1, keepdims=True))
    w = jnp.exp(s - top)
    back = jnp.exp(near_top - top)
    total = back * near_total + jnp.sum(w, axis=1, keepdims=True)
    acc = back * acc_ref[0] + jnp.dot(
        w.astype(jnp.bfloat16), v_ref[...], preferred_element_type=jnp.float32
    )
    res = (acc / total).astype(jnp.bfloat16)
    for h in range(GROUP):
        out_ref[:, h * WIDTH : (h + 1) * WIDTH] = res[h * BLOCK : (h + 1) * BLOCK]


def far_attention(live, queries, far, acc, stat):
    return pl.pallas_call(
        far_kernel,
        grid_spec=pltpu.PrefetchScalarGridSpec(
            num_scalar_prefetch=1,
            grid=(KEY_HEADS,),
            in_specs=[
                pl.BlockSpec((BLOCK, GROUP * WIDTH), lambda e, live: (0, e)),
                pl.BlockSpec((LIST * BLOCK, WIDTH), lambda e, live: (0, 2 * e)),
                pl.BlockSpec((LIST * BLOCK, WIDTH), lambda e, live: (0, 2 * e + 1)),
                pl.BlockSpec((1, QROWS, WIDTH), lambda e, live: (e, 0, 0)),
                pl.BlockSpec((1, QROWS, WIDTH), lambda e, live: (e, 0, 0)),
            ],
            out_specs=pl.BlockSpec((BLOCK, GROUP * WIDTH), lambda e, live: (0, e)),
        ),
        out_shape=jax.ShapeDtypeStruct((BLOCK, KEY_HEADS * GROUP * WIDTH), jnp.bfloat16),
        compiler_params=pltpu.CompilerParams(vmem_limit_bytes=40 * 1024 * 1024),
        name="far",
    )(live, queries, far, far, acc, stat)


def pick_kernel(index_ref, *refs):
    units, out_ref = refs[:-1], refs[-1]
    picked_rows = LAYER * LIST * SHARE
    lane = lax.broadcasted_iota(jnp.int32, (picked_rows, UNIT * Z), 1)
    for e in range(KEY_HEADS):
        hot = jnp.where(lane == index_ref[:, e : e + 1], 1.0, 0.0).astype(jnp.bfloat16)
        lanes = slice(2 * WIDTH * e, 2 * WIDTH * (e + 1))
        table = jnp.concatenate([u[:, lanes] for u in units], axis=0)
        out_ref[:, lanes] = jnp.dot(hot, table, preferred_element_type=jnp.float32).astype(
            jnp.bfloat16
        )


def pick(index, units):
    return pl.pallas_call(
        pick_kernel,
        out_shape=jax.ShapeDtypeStruct((LAYER * LIST * SHARE, LANES), jnp.bfloat16),
        compiler_params=pltpu.CompilerParams(vmem_limit_bytes=40 * 1024 * 1024),
        name="pick",
    )(index, *units)


def local(queries, keys, values, far_blocks, far_live_length):
    z = lax.axis_index("z")
    both = jnp.stack(
        [keys.reshape(KDEV, KEY_HEADS, WIDTH), values.reshape(KDEV, KEY_HEADS, WIDTH)], axis=2
    ).reshape(KDEV, LANES)
    near = lax.all_gather(both, ("y", "x"), axis=0, tiled=True)

    ids = far_blocks.reshape(1, KEY_HEADS * LIST).astype(jnp.bfloat16)
    ids = jnp.broadcast_to(jnp.pad(ids, ((0, 0), (0, WIDTH - KEY_HEADS * LIST))), (KDEV, WIDTH))
    sent = jnp.concatenate([both, ids], axis=1).reshape(LAYER, ROWS, LANES + WIDTH)
    got = lax.all_to_all(sent, ("c", "y", "x"), 0, 0, tiled=True)
    unit = got[:, :, :LANES].reshape(UNIT, LANES)
    asked = got[:, 0, LANES : LANES + KEY_HEADS * LIST].astype(jnp.int32)

    ups = [unit]
    downs = [unit]
    up = [(k, (k + 1) % Z) for k in range(Z)]
    down = [(k, (k - 1) % Z) for k in range(Z)]
    for step in range(Z // 2):
        ups.append(lax.ppermute(ups[-1], "z", up))
        if step < Z // 2 - 1:
            downs.append(lax.ppermute(downs[-1], "z", down))
    units = downs + ups[:0:-1]

    asked = asked.reshape(LAYER, KEY_HEADS, LIST, 1)
    place = (asked // (C * 8) - z) % Z
    row = (place * (C * 8) + asked % (C * 8)) * SHARE + jnp.arange(SHARE, dtype=jnp.int32)
    index = row.transpose(0, 2, 3, 1).reshape(LAYER * LIST * SHARE, KEY_HEADS)

    picked = pick(index, units)
    picked, queries = lax.optimization_barrier((picked, queries))
    arrived = lax.all_to_all(
        picked.reshape(LAYER, LIST * SHARE, LANES), ("c", "y", "x"), 0, 0, tiled=True
    )
    acc, stat = near_attention(queries, near)
    live = far_live_length.reshape(KEY_HEADS)
    return far_attention(live, queries, arrived.reshape(LIST * BLOCK, LANES), acc, stat)


def solution(mesh):
    fine = Mesh(mesh.devices.reshape(Z, C, Y, X), ("z", "c", "y", "x"))
    axes = ("z", "c", "y", "x")
    placed = (
        P(axes, None),
        P(axes, None),
        P(axes, None),
        P(axes, None, None),
        P(axes, None),
    )
    return jax.shard_map(
        local, mesh=fine, in_specs=placed, out_specs=P(axes, None), check_vma=False
    )
```

time: 389 us -> 141 us (0.36)
  waiting for transfers between devices: 179 us -> 15.5 us
  blocking collectives: 143 us -> 17.3 us
  starting transfers between devices: 5.03 us -> 64.9 us
  Pallas kernels: 0 us -> 20.9 us
  local copies, waits for them, and re-layouts: 24.7 us -> 7.14 us
  matrix products: 13.8 us -> 0 us
  other arithmetic: 9.08 us -> 0.63 us
    all_to_all x2 -> x1, blocking collectives: 143 us -> 17.3 us  [local(): got = lax.all_to_all(sent, ('c', 'y', 'x'), 0, 0, tiled=True)]
    all_gather x2 -> x1, waiting for transfers between devices: 92 us -> 0.02 us  [local(): near = lax.all_gather(both, ('y', 'x'), axis=0, tiled=True)]
    all_to_all x1, waiting for transfers between devices: 85.5 us -> 5.42 us  [local(): lax.all_to_all(picked.reshape(LAYER, LIST * SHARE, LANES), ('c', 'y', 'x'...]
    ppermute x0 -> x15, starting transfers between devices: none -> 52.6 us  [the longest x7 36.9 us: local(): downs.append(lax.ppermute(downs[-1], 'z', down))]
    pallas_call x0 -> x3, Pallas kernels: none -> 20.9 us  [the longest x1 10.2 us: far_attention(): pl.pallas_call(far_kernel, grid_spec=pltpu.PrefetchScalarGridSpec(num_sca...]
    dot_general x16 -> x0, matrix products: 13.8 us -> none  [the longest x4 7.6 us: attend_all(): jnp.einsum('bqgd,kd->bgqk', query_h, near_key_rows3[:, head_slot], prefer...]
    gather x4 -> x0, local copies, waits for them, and re-layouts: 10.3 us -> none  [the longest x1 3.02 us: local(): jnp.take(flattened_keys, source_device, axis=0)]
    ppermute x0 -> x15, waiting for transfers between devices: none -> 10 us  [the longest x8 10 us: local(): ups.append(lax.ppermute(ups[-1], 'z', up))]
  transfers between devices with their start and end apart: 3 -> 17, of which waited for: 3 -> 9; matrix products, arithmetic and copies ran while one was open for 5% -> 1% of each run, Pallas kernels for 0% -> 8%
where the time goes in v1:
time: 141 us; the launch traced here: 140 us
  starting transfers between devices  64.9 us (46%)
  Pallas kernels  20.9 us (15%)
  blocking collectives  17.3 us (12%)
  waiting for transfers between devices  15.5 us (11%)
  between operations  13.7 us (10%)
  local copies, waits for them, and re-layouts  7.14 us (5%)
    ppermute x7, starting transfers between devices, local(): downs.append(lax.ppermute(downs[-1], 'z', down))  36.9 us
    all_to_all x1, blocking collectives, local(): got = lax.all_to_all(sent, ('c', 'y', 'x'), 0, 0, tiled=True)  17.3 us
    ppermute x8, starting transfers between devices, local(): ups.append(lax.ppermute(ups[-1], 'z', up))  15.7 us
    all_to_all x1, starting transfers between devices, local(): lax.all_to_all(picked.reshape(LAYER, LIST * SHARE, LANES), ('c', 'y', 'x'...  12.3 us
    pallas_call x1, Pallas kernels, far_attention(): pl.pallas_call(far_kernel, grid_spec=pltpu.PrefetchScalarGridSpec(num_sca...  10.2 us
    ppermute x8, waiting for transfers between devices, local(): ups.append(lax.ppermute(ups[-1], 'z', up))  10 us
    pallas_call x1, Pallas kernels, near_attention(): pl.pallas_call(near_kernel, grid=(KEY_HEADS,), in_specs=[pl.BlockSpec((BL...  8.38 us
    all_to_all x1, waiting for transfers between devices, local(): lax.all_to_all(picked.reshape(LAYER, LIST * SHARE, LANES), ('c', 'y', 'x'...  5.42 us
  transfers between devices with their start and end apart: 17, of which 9 were waited for; matrix products, arithmetic and copies ran while one was open for 1% of the time, Pallas kernels for 8%

profile of v1, /device:TPU:1, one launch (start us, length us, event | category | flops | bytes accessed | tf_op | source)
XLA Modules:
  0.0 140.1 jit_solution(13030142688152898621)
XLA Ops:
  6.5 0.9 stack_reshape.8
  7.4 0.9 stack_reshape.9
  8.6 0.7 reshape.150
  9.7 17.3 %all_to_all.10 = bf16[32,2,1152]{2,1,0:T(2,128)(2,1)S(1)} all-to-all(bf16[32,2,1152]{2,1,0:T(2,128)(2,1)S(1)} %pad_maximum_fusion), channel_id=1, replica_groups=mesh['z'=16,'c'=2,'y'=4,'x'=4] {'c','y','x'}, dimensions={0} | all-to-all | bytes 294912 | tf_op jit(solution)/shard_map/all_to_all | solution.py:147
  27.1 2.3 %collective-permute-start.7 = (bf16[64,1024]{1,0:T(8,128)(2,1)S(1)}, bf16[64,1024]{1,0:T(8,128)(2,1)S(1)}, u32[]{:S(2)}, u32[]{:S(2)}) collective-permute-start(bf16[64,1024]{1,0:T(8,128)(2,1)S(1)} %reshape.147.refs_0_), channel_id=1, source_target_pairs={{0,32},{32,64},{64,96},{96,128},{128,160},{160,192},{192,224},{224... | collective-permute-start | bytes 393224 | tf_op jit(solution)/shard_map/ppermute | solution.py:156
  29.5 9.5 %collective-permute-start = (bf16[64,1024]{1,0:T(8,128)(2,1)S(1)}, bf16[64,1024]{1,0:T(8,128)(2,1)S(1)}, u32[]{:S(2)}, u32[]{:S(2)}) collective-permute-start(bf16[64,1024]{1,0:T(8,128)(2,1)S(1)} %reshape.147.refs_0_), channel_id=1, source_target_pairs={{0,480},{32,0},{64,32},{96,64},{128,96},{160,128},{192,160},{224,1... | collective-permute-start | bytes 393224 | tf_op jit(solution)/shard_map/ppermute | solution.py:158
  39.0 1.4 %collective-permute-done.7.refs_15_ = bf16[64,1024]{1,0:T(8,128)(2,1)S(1)} collective-permute-done((bf16[64,1024]{1,0:T(8,128)(2,1)S(1)}, bf16[64,1024]{1,0:T(8,128)(2,1)S(1)}, u32[]{:S(2)}, u32[]{:S(2)}) %collective-permute-start.7) | collective-permute-done | bytes 131104 | tf_op jit(solution)/shard_map/ppermute | solution.py:156
  40.4 1.9 %collective-permute-start.8 = (bf16[64,1024]{1,0:T(8,128)(2,1)S(1)}, bf16[64,1024]{1,0:T(8,128)(2,1)S(1)}, u32[]{:S(2)}, u32[]{:S(2)}) collective-permute-start(bf16[64,1024]{1,0:T(8,128)(2,1)S(1)} %collective-permute-done.7.refs_15_), channel_id=1, source_target_pairs={{0,32},{32,64},{64,96},{96,128},{128,160},{160,192},{192,224},{224... | collective-permute-start | bytes 393224 | tf_op jit(solution)/shard_map/ppermute | solution.py:156
  42.3 4.6 %collective-permute-start.1 = (bf16[64,1024]{1,0:T(8,128)(2,1)S(1)}, bf16[64,1024]{1,0:T(8,128)(2,1)S(1)}, u32[]{:S(2)}, u32[]{:S(2)}) collective-permute-start(bf16[64,1024]{1,0:T(8,128)(2,1)S(1)} %collective-permute-done.refs_1_), channel_id=1, source_target_pairs={{0,480},{32,0},{64,32},{96,64},{128,96},{160,128},{192,160},{224,1... | collective-permute-start | bytes 393224 | tf_op jit(solution)/shard_map/ppermute | solution.py:158
  46.9 0.4 collective-permute-done.8.refs_14_
  47.3 1.9 %collective-permute-start.9 = (bf16[64,1024]{1,0:T(8,128)(2,1)S(1)}, bf16[64,1024]{1,0:T(8,128)(2,1)S(1)}, u32[]{:S(2)}, u32[]{:S(2)}) collective-permute-start(bf16[64,1024]{1,0:T(8,128)(2,1)S(1)} %collective-permute-done.8.refs_14_), channel_id=1, source_target_pairs={{0,32},{32,64},{64,96},{96,128},{128,160},{160,192},{192,224},{224... | collective-permute-start | bytes 393224 | tf_op jit(solution)/shard_map/ppermute | solution.py:156
  49.2 4.6 %collective-permute-start.2 = (bf16[64,1024]{1,0:T(8,128)(2,1)S(1)}, bf16[64,1024]{1,0:T(8,128)(2,1)S(1)}, u32[]{:S(2)}, u32[]{:S(2)}) collective-permute-start(bf16[64,1024]{1,0:T(8,128)(2,1)S(1)} %collective-permute-done.1.refs_2_), channel_id=1, source_target_pairs={{0,480},{32,0},{64,32},{96,64},{128,96},{160,128},{192,160},{224,1... | collective-permute-start | bytes 393224 | tf_op jit(solution)/shard_map/ppermute | solution.py:158
  54.2 1.9 %collective-permute-start.10 = (bf16[64,1024]{1,0:T(8,128)(2,1)S(1)}, bf16[64,1024]{1,0:T(8,128)(2,1)S(1)}, u32[]{:S(2)}, u32[]{:S(2)}) collective-permute-start(bf16[64,1024]{1,0:T(8,128)(2,1)S(1)} %collective-permute-done.9.refs_13_), channel_id=1, source_target_pairs={{0,32},{32,64},{64,96},{96,128},{128,160},{160,192},{192,224},{224... | collective-permute-start | bytes 393224 | tf_op jit(solution)/shard_map/ppermute | solution.py:156
  56.1 4.6 %collective-permute-start.3 = (bf16[64,1024]{1,0:T(8,128)(2,1)S(1)}, bf16[64,1024]{1,0:T(8,128)(2,1)S(1)}, u32[]{:S(2)}, u32[]{:S(2)}) collective-permute-start(bf16[64,1024]{1,0:T(8,128)(2,1)S(1)} %collective-permute-done.2.refs_3_), channel_id=1, source_target_pairs={{0,480},{32,0},{64,32},{96,64},{128,96},{160,128},{192,160},{224,1... | collective-permute-start | bytes 393224 | tf_op jit(solution)/shard_map/ppermute | solution.py:158
  61.1 1.9 %collective-permute-start.11 = (bf16[64,1024]{1,0:T(8,128)(2,1)S(1)}, bf16[64,1024]{1,0:T(8,128)(2,1)S(1)}, u32[]{:S(2)}, u32[]{:S(2)}) collective-permute-start(bf16[64,1024]{1,0:T(8,128)(2,1)S(1)} %collective-permute-done.10.refs_12_), channel_id=1, source_target_pairs={{0,32},{32,64},{64,96},{96,128},{128,160},{160,192},{192,224},{224... | collective-permute-start | bytes 393224 | tf_op jit(solution)/shard_map/ppermute | solution.py:156
  63.1 4.6 %collective-permute-start.4 = (bf16[64,1024]{1,0:T(8,128)(2,1)S(1)}, bf16[64,1024]{1,0:T(8,128)(2,1)S(1)}, u32[]{:S(2)}, u32[]{:S(2)}) collective-permute-start(bf16[64,1024]{1,0:T(8,128)(2,1)S(1)} %collective-permute-done.3.refs_4_), channel_id=1, source_target_pairs={{0,480},{32,0},{64,32},{96,64},{128,96},{160,128},{192,160},{224,1... | collective-permute-start | bytes 393224 | tf_op jit(solution)/shard_map/ppermute | solution.py:158
  67.6 0.8 collective-permute-done.11.refs_11_
  68.4 1.9 %collective-permute-start.12 = (bf16[64,1024]{1,0:T(8,128)(2,1)S(1)}, bf16[64,1024]{1,0:T(8,128)(2,1)S(1)}, u32[]{:S(2)}, u32[]{:S(2)}) collective-permute-start(bf16[64,1024]{1,0:T(8,128)(2,1)S(1)} %collective-permute-done.11.refs_11_), channel_id=1, source_target_pairs={{0,32},{32,64},{64,96},{96,128},{128,160},{160,192},{192,224},{224... | collective-permute-start | bytes 393224 | tf_op jit(solution)/shard_map/ppermute | solution.py:156
  70.6 4.6 %collective-permute-start.5 = (bf16[64,1024]{1,0:T(8,128)(2,1)S(1)}, bf16[64,1024]{1,0:T(8,128)(2,1)S(1)}, u32[]{:S(2)}, u32[]{:S(2)}) collective-permute-start(bf16[64,1024]{1,0:T(8,128)(2,1)S(1)} %collective-permute-done.4.refs_5_), channel_id=1, source_target_pairs={{0,480},{32,0},{64,32},{96,64},{128,96},{160,128},{192,160},{224,1... | collective-permute-start | bytes 393224 | tf_op jit(solution)/shard_map/ppermute | solution.py:158
  75.2 0.6 collective-permute-done.12.refs_10_
  75.8 1.9 %collective-permute-start.13 = (bf16[64,1024]{1,0:T(8,128)(2,1)S(1)}, bf16[64,1024]{1,0:T(8,128)(2,1)S(1)}, u32[]{:S(2)}, u32[]{:S(2)}) collective-permute-start(bf16[64,1024]{1,0:T(8,128)(2,1)S(1)} %collective-permute-done.12.refs_10_), channel_id=1, source_target_pairs={{0,32},{32,64},{64,96},{96,128},{128,160},{160,192},{192,224},{224... | collective-permute-start | bytes 393224 | tf_op jit(solution)/shard_map/ppermute | solution.py:156
  77.8 4.6 %collective-permute-start.6 = (bf16[64,1024]{1,0:T(8,128)(2,1)S(1)}, bf16[64,1024]{1,0:T(8,128)(2,1)S(1)}, u32[]{:S(2)}, u32[]{:S(2)}) collective-permute-start(bf16[64,1024]{1,0:T(8,128)(2,1)S(1)} %collective-permute-done.5.refs_6_), channel_id=1, source_target_pairs={{0,480},{32,0},{64,32},{96,64},{128,96},{160,128},{192,160},{224,1... | collective-permute-start | bytes 393224 | tf_op jit(solution)/shard_map/ppermute | solution.py:158
  82.7 1.9 %collective-permute-start.14 = (bf16[64,1024]{1,0:T(8,128)(2,1)S(1)}, bf16[64,1024]{1,0:T(8,128)(2,1)S(1)}, u32[]{:S(2)}, u32[]{:S(2)}) collective-permute-start(bf16[64,1024]{1,0:T(8,128)(2,1)S(1)} %collective-permute-done.13.refs_9_), channel_id=1, source_target_pairs={{0,32},{32,64},{64,96},{96,128},{128,160},{160,192},{192,224},{224... | collective-permute-start | bytes 393224 | tf_op jit(solution)/shard_map/ppermute | solution.py:156
  84.8 5.8 %collective-permute-done.14.refs_8_ = bf16[64,1024]{1,0:T(8,128)(2,1)S(1)} collective-permute-done((bf16[64,1024]{1,0:T(8,128)(2,1)S(1)}, bf16[64,1024]{1,0:T(8,128)(2,1)S(1)}, u32[]{:S(2)}, u32[]{:S(2)}) %collective-permute-start.14) | collective-permute-done | bytes 131104 | tf_op jit(solution)/shard_map/ppermute | solution.py:156
  90.6 2.3 %pick.1 = bf16[512,1024]{1,0:T(8,128)(2,1)} custom-call(s32[512,4]{1,0:T(8,128)S(1)} %broadcast_add_fusion.index_ref, bf16[64,1024]{1,0:T(8,128)(2,1)S(1)} %reshape.147.refs_0_, bf16[64,1024]{1,0:T(8,128)(2,1)S(1)} %collective-permute-done.refs_1_, bf16[64,1024]{1,0:T(8,128)(2,1)S(1)} %collective-permute-done.1.refs_2_, ...), custom_call_target="tpu_custom_call" | custom-call | tf_op jit(solution)/shard_map/pick/pallas_call | solution.py:129
  92.9 12.3 %all-to-all-start.1 = ((bf16[32,16,1024]{2,1,0:T(8,128)(2,1)}), bf16[32,16,1024]{2,1,0:T(8,128)(2,1)S(1)}, u32[]{:S(2)}, u32[]{:S(2)}) async-start(bf16[32,16,1024]{2,1,0:T(8,128)(2,1)} %bitcast.6), calls=%async_computation.1 | async-start | bytes 2097152 | tf_op jit(solution)/shard_map/all_to_all | solution.py:168
  105.2 1.6 %copy-done.4 = bf16[1024,1024]{1,0:T(8,128)(2,1)S(1)} copy-done((bf16[1024,1024]{1,0:T(8,128)(2,1)S(1)}, bf16[1024,1024]{1,0:T(8,128)(2,1)}, u32[]{:S(2)}) %copy-start.4) | copy-done | bytes 2097176
  106.8 8.4 %near.1 = (f32[4,640,128]{2,1,0:T(8,128)S(1)}, f32[4,640,128]{2,1,0:T(8,128)S(1)}) custom-call(bf16[128,2560]{1,0:T(8,128)(2,1)S(1)} %copy-done.2, bf16[1024,1024]{1,0:T(8,128)(2,1)S(1)} %copy-done.4, bf16[1024,1024]{1,0:T(8,128)(2,1)S(1)} %copy-done.4), custom_call_target="tpu_custom_call" | custom-call | flops 1342177280 | bytes 8388608 | tf_op jit(solution)/shard_map/near/pallas_call | solution.py:46
  115.2 1.1 copy-done
  116.3 5.4 %all-to-all-done.1 = bf16[32,16,1024]{2,1,0:T(8,128)(2,1)S(1)} async-done(((bf16[32,16,1024]{2,1,0:T(8,128)(2,1)}), bf16[32,16,1024]{2,1,0:T(8,128)(2,1)S(1)}, u32[]{:S(2)}, u32[]{:S(2)}) %all-to-all-start.1) | async-done | bytes 1048608 | tf_op jit(solution)/shard_map/all_to_all | solution.py:168
  121.7 1.3 copy-done.1
  123.0 10.2 %far.1 = bf16[128,2560]{1,0:T(8,128)(2,1)} custom-call(s32[4]{0:T(128)S(1)} %bitcast.12, bf16[128,2560]{1,0:T(8,128)(2,1)S(1)} %copy-done.2, bf16[512,1024]{1,0:T(8,128)(2,1)S(1)} %bitcast.10, bf16[512,1024]{1,0:T(8,128)(2,1)S(1)} %bitcast.11, f32[4,640,128]{2,1,0:T(8,128)S(1)} %get-tuple-element.11.acc_ref, f32[4,640,128]{2,1,0:T(8,128)S(1)} %copy-done.1), custom_call_target="tpu_custom_call" | custom-call | tf_op jit(solution)/shard_map/far/pallas_call | solution.py:95
  (39 shorter events, 2.4 us)
Async XLA Ops:
  6.5 2.9 %copy-start.5 = (s32[1,4,4]{2,1,0:T(4,128)S(1)}, s32[1,4,4]{2,1,0:T(4,128)}, u32[]{:S(2)}) copy-start(s32[1,4,4]{2,1,0:T(4,128)} %param.8) | copy-start | bytes 196
  6.5 98.7 %all-gather.2.cloned.1.call-start = ((), (), s32[]{:S(2)}) async-start(), calls=%async_computation.2 | async-start | bytes 2228224 | tf_op jit(solution)/shard_map/all_gather | solution.py:142
  27.1 13.3 %collective-permute-start.7 = (bf16[64,1024]{1,0:T(8,128)(2,1)S(1)}, bf16[64,1024]{1,0:T(8,128)(2,1)S(1)}, u32[]{:S(2)}, u32[]{:S(2)}) collective-permute-start(bf16[64,1024]{1,0:T(8,128)(2,1)S(1)} %reshape.147.refs_0_), channel_id=1, source_target_pairs={{0,32},{32,64},{64,96},{96,128},{128,160},{160,192},{192,224},{224... | collective-permute-start | bytes 393224 | tf_op jit(solution)/shard_map/ppermute | solution.py:156
  29.5 12.9 %collective-permute-start = (bf16[64,1024]{1,0:T(8,128)(2,1)S(1)}, bf16[64,1024]{1,0:T(8,128)(2,1)S(1)}, u32[]{:S(2)}, u32[]{:S(2)}) collective-permute-start(bf16[64,1024]{1,0:T(8,128)(2,1)S(1)} %reshape.147.refs_0_), channel_id=1, source_target_pairs={{0,480},{32,0},{64,32},{96,64},{128,96},{160,128},{192,160},{224,1... | collective-permute-start | bytes 393224 | tf_op jit(solution)/shard_map/ppermute | solution.py:158
  40.4 6.9 %collective-permute-start.8 = (bf16[64,1024]{1,0:T(8,128)(2,1)S(1)}, bf16[64,1024]{1,0:T(8,128)(2,1)S(1)}, u32[]{:S(2)}, u32[]{:S(2)}) collective-permute-start(bf16[64,1024]{1,0:T(8,128)(2,1)S(1)} %collective-permute-done.7.refs_15_), channel_id=1, source_target_pairs={{0,32},{32,64},{64,96},{96,128},{128,160},{160,192},{192,224},{224... | collective-permute-start | bytes 393224 | tf_op jit(solution)/shard_map/ppermute | solution.py:156
  42.3 6.9 %collective-permute-start.1 = (bf16[64,1024]{1,0:T(8,128)(2,1)S(1)}, bf16[64,1024]{1,0:T(8,128)(2,1)S(1)}, u32[]{:S(2)}, u32[]{:S(2)}) collective-permute-start(bf16[64,1024]{1,0:T(8,128)(2,1)S(1)} %collective-permute-done.refs_1_), channel_id=1, source_target_pairs={{0,480},{32,0},{64,32},{96,64},{128,96},{160,128},{192,160},{224,1... | collective-permute-start | bytes 393224 | tf_op jit(solution)/shard_map/ppermute | solution.py:158
  47.3 6.9 %collective-permute-start.9 = (bf16[64,1024]{1,0:T(8,128)(2,1)S(1)}, bf16[64,1024]{1,0:T(8,128)(2,1)S(1)}, u32[]{:S(2)}, u32[]{:S(2)}) collective-permute-start(bf16[64,1024]{1,0:T(8,128)(2,1)S(1)} %collective-permute-done.8.refs_14_), channel_id=1, source_target_pairs={{0,32},{32,64},{64,96},{96,128},{128,160},{160,192},{192,224},{224... | collective-permute-start | bytes 393224 | tf_op jit(solution)/shard_map/ppermute | solution.py:156
  49.2 6.9 %collective-permute-start.2 = (bf16[64,1024]{1,0:T(8,128)(2,1)S(1)}, bf16[64,1024]{1,0:T(8,128)(2,1)S(1)}, u32[]{:S(2)}, u32[]{:S(2)}) collective-permute-start(bf16[64,1024]{1,0:T(8,128)(2,1)S(1)} %collective-permute-done.1.refs_2_), channel_id=1, source_target_pairs={{0,480},{32,0},{64,32},{96,64},{128,96},{160,128},{192,160},{224,1... | collective-permute-start | bytes 393224 | tf_op jit(solution)/shard_map/ppermute | solution.py:158
  54.2 6.9 %collective-permute-start.10 = (bf16[64,1024]{1,0:T(8,128)(2,1)S(1)}, bf16[64,1024]{1,0:T(8,128)(2,1)S(1)}, u32[]{:S(2)}, u32[]{:S(2)}) collective-permute-start(bf16[64,1024]{1,0:T(8,128)(2,1)S(1)} %collective-permute-done.9.refs_13_), channel_id=1, source_target_pairs={{0,32},{32,64},{64,96},{96,128},{128,160},{160,192},{192,224},{224... | collective-permute-start | bytes 393224 | tf_op jit(solution)/shard_map/ppermute | solution.py:156
  56.1 6.9 %collective-permute-start.3 = (bf16[64,1024]{1,0:T(8,128)(2,1)S(1)}, bf16[64,1024]{1,0:T(8,128)(2,1)S(1)}, u32[]{:S(2)}, u32[]{:S(2)}) collective-permute-start(bf16[64,1024]{1,0:T(8,128)(2,1)S(1)} %collective-permute-done.2.refs_3_), channel_id=1, source_target_pairs={{0,480},{32,0},{64,32},{96,64},{128,96},{160,128},{192,160},{224,1... | collective-permute-start | bytes 393224 | tf_op jit(solution)/shard_map/ppermute | solution.py:158
  61.1 7.3 %collective-permute-start.11 = (bf16[64,1024]{1,0:T(8,128)(2,1)S(1)}, bf16[64,1024]{1,0:T(8,128)(2,1)S(1)}, u32[]{:S(2)}, u32[]{:S(2)}) collective-permute-start(bf16[64,1024]{1,0:T(8,128)(2,1)S(1)} %collective-permute-done.10.refs_12_), channel_id=1, source_target_pairs={{0,32},{32,64},{64,96},{96,128},{128,160},{160,192},{192,224},{224... | collective-permute-start | bytes 393224 | tf_op jit(solution)/shard_map/ppermute | solution.py:156
  63.1 7.5 %collective-permute-start.4 = (bf16[64,1024]{1,0:T(8,128)(2,1)S(1)}, bf16[64,1024]{1,0:T(8,128)(2,1)S(1)}, u32[]{:S(2)}, u32[]{:S(2)}) collective-permute-start(bf16[64,1024]{1,0:T(8,128)(2,1)S(1)} %collective-permute-done.3.refs_4_), channel_id=1, source_target_pairs={{0,480},{32,0},{64,32},{96,64},{128,96},{160,128},{192,160},{224,1... | collective-permute-start | bytes 393224 | tf_op jit(solution)/shard_map/ppermute | solution.py:158
  68.4 7.3 %collective-permute-start.12 = (bf16[64,1024]{1,0:T(8,128)(2,1)S(1)}, bf16[64,1024]{1,0:T(8,128)(2,1)S(1)}, u32[]{:S(2)}, u32[]{:S(2)}) collective-permute-start(bf16[64,1024]{1,0:T(8,128)(2,1)S(1)} %collective-permute-done.11.refs_11_), channel_id=1, source_target_pairs={{0,32},{32,64},{64,96},{96,128},{128,160},{160,192},{192,224},{224... | collective-permute-start | bytes 393224 | tf_op jit(solution)/shard_map/ppermute | solution.py:156
  70.6 7.2 %collective-permute-start.5 = (bf16[64,1024]{1,0:T(8,128)(2,1)S(1)}, bf16[64,1024]{1,0:T(8,128)(2,1)S(1)}, u32[]{:S(2)}, u32[]{:S(2)}) collective-permute-start(bf16[64,1024]{1,0:T(8,128)(2,1)S(1)} %collective-permute-done.4.refs_5_), channel_id=1, source_target_pairs={{0,480},{32,0},{64,32},{96,64},{128,96},{160,128},{192,160},{224,1... | collective-permute-start | bytes 393224 | tf_op jit(solution)/shard_map/ppermute | solution.py:158
  75.8 6.9 %collective-permute-start.13 = (bf16[64,1024]{1,0:T(8,128)(2,1)S(1)}, bf16[64,1024]{1,0:T(8,128)(2,1)S(1)}, u32[]{:S(2)}, u32[]{:S(2)}) collective-permute-start(bf16[64,1024]{1,0:T(8,128)(2,1)S(1)} %collective-permute-done.12.refs_10_), channel_id=1, source_target_pairs={{0,32},{32,64},{64,96},{96,128},{128,160},{160,192},{192,224},{224... | collective-permute-start | bytes 393224 | tf_op jit(solution)/shard_map/ppermute | solution.py:156
  77.8 6.9 %collective-permute-start.6 = (bf16[64,1024]{1,0:T(8,128)(2,1)S(1)}, bf16[64,1024]{1,0:T(8,128)(2,1)S(1)}, u32[]{:S(2)}, u32[]{:S(2)}) collective-permute-start(bf16[64,1024]{1,0:T(8,128)(2,1)S(1)} %collective-permute-done.5.refs_6_), channel_id=1, source_target_pairs={{0,480},{32,0},{64,32},{96,64},{128,96},{160,128},{192,160},{224,1... | collective-permute-start | bytes 393224 | tf_op jit(solution)/shard_map/ppermute | solution.py:158
  82.7 7.9 %collective-permute-start.14 = (bf16[64,1024]{1,0:T(8,128)(2,1)S(1)}, bf16[64,1024]{1,0:T(8,128)(2,1)S(1)}, u32[]{:S(2)}, u32[]{:S(2)}) collective-permute-start(bf16[64,1024]{1,0:T(8,128)(2,1)S(1)} %collective-permute-done.13.refs_9_), channel_id=1, source_target_pairs={{0,32},{32,64},{64,96},{96,128},{128,160},{160,192},{192,224},{224... | collective-permute-start | bytes 393224 | tf_op jit(solution)/shard_map/ppermute | solution.py:156
  92.9 12.3 %copy-start.2 = (bf16[128,2560]{1,0:T(8,128)(2,1)S(1)}, bf16[128,2560]{1,0:T(8,128)(2,1)}, u32[]{:S(2)}) copy-start(bf16[128,2560]{1,0:T(8,128)(2,1)} %q_ref.1) | copy-start | bytes 1966084
  92.9 28.8 %all-to-all-start.1 = ((bf16[32,16,1024]{2,1,0:T(8,128)(2,1)}), bf16[32,16,1024]{2,1,0:T(8,128)(2,1)S(1)}, u32[]{:S(2)}, u32[]{:S(2)}) async-start(bf16[32,16,1024]{2,1,0:T(8,128)(2,1)} %bitcast.6), calls=%async_computation.1 | async-start | bytes 2097152 | tf_op jit(solution)/shard_map/all_to_all | solution.py:168
  105.2 16.5 %copy-start.3 = (s32[1,4]{1,0:T(1,128)S(1)}, s32[1,4]{1,0:T(1,128)}, u32[]{:S(2)}) copy-start(s32[1,4]{1,0:T(1,128)} %param.9) | copy-start | bytes 52
  105.2 1.6 %copy-start.4 = (bf16[1024,1024]{1,0:T(8,128)(2,1)S(1)}, bf16[1024,1024]{1,0:T(8,128)(2,1)}, u32[]{:S(2)}) copy-start(bf16[1024,1024]{1,0:T(8,128)(2,1)} %all-gather.2.cloned.1.call-done.k_ref.v_ref) | copy-start | bytes 6291460
  115.2 1.1 copy-start
  121.7 1.3 copy-start.1
Sparse Core Ops, SparseCore 0:
  10.4 64.6 all-gather.1

commit v2 on v1

v2 whole, which is shorter than its diff:
```python
import functools
import math

import jax
import jax.numpy as jnp
from jax import lax
from jax.experimental import pallas as pl
from jax.experimental.pallas import tpu as pltpu
from jax.sharding import Mesh, PartitionSpec as P

KEY_HEADS = 4
GROUP = 5
WIDTH = 128
BLOCK = 128
LIST = 4
ZH, ZL, C, Y, X = 8, 2, 2, 4, 4
PEERS = ZL * C * Y * X
PEER_AXES = ("zl", "c", "y", "x")
KDEV = 64
SHARE = 2
NEAR = Y * X * KDEV
LANES = KEY_HEADS * 2 * WIDTH
HALF = LANES // 2
UNIT = PEERS * SHARE
MAIN = UNIT - 16
REST = UNIT - MAIN
BLOCKS_PAIR = 32
PICKED = PEERS * LIST * SHARE
SCALE_LOG2 = math.log2(math.e) / math.sqrt(WIDTH)
MIB = 1024 * 1024
QROWS = GROUP * BLOCK


def stack_heads(q_ref):
    return jnp.concatenate([q_ref[:, h * WIDTH : (h + 1) * WIDTH] for h in range(GROUP)], axis=0)


def near_kernel(q_ref, k_ref, v_ref, acc_ref, stat_ref):
    q = stack_heads(q_ref)
    s = lax.dot_general(
        q, k_ref[...], (((1,), (1,)), ((), ())), preferred_element_type=jnp.float32
    )
    top = jnp.max(s, axis=1, keepdims=True)
    w = jnp.exp2((s - top) * SCALE_LOG2)
    total = jnp.sum(w, axis=1, keepdims=True)
    acc_ref[0] = jnp.dot(w.astype(jnp.bfloat16), v_ref[...], preferred_element_type=jnp.float32)
    lane = lax.broadcasted_iota(jnp.int32, (QROWS, WIDTH), 1)
    stat_ref[0] = jnp.where(lane == 0, top, total)


def near_attention(queries, near):
    return pl.pallas_call(
        near_kernel,
        grid=(KEY_HEADS,),
        in_specs=[
            pl.BlockSpec((BLOCK, GROUP * WIDTH), lambda e: (0, e)),
            pl.BlockSpec((NEAR, WIDTH), lambda e: (0, 2 * e)),
            pl.BlockSpec((NEAR, WIDTH), lambda e: (0, 2 * e + 1)),
        ],
        out_specs=[
            pl.BlockSpec((1, QROWS, WIDTH), lambda e: (e, 0, 0)),
            pl.BlockSpec((1, QROWS, WIDTH), lambda e: (e, 0, 0)),
        ],
        out_shape=[
            jax.ShapeDtypeStruct((KEY_HEADS, QROWS, WIDTH), jnp.float32),
            jax.ShapeDtypeStruct((KEY_HEADS, QROWS, WIDTH), jnp.float32),
        ],
        compiler_params=pltpu.CompilerParams(vmem_limit_bytes=16 * MIB),
        cost_estimate=pl.CostEstimate(
            flops=4 * KEY_HEADS * QROWS * NEAR * WIDTH,
            bytes_accessed=8 * 1024 * 1024,
            transcendentals=KEY_HEADS * QROWS * NEAR,
        ),
        name="near",
    )(queries, near, near)


def far_kernel(live_ref, q_ref, far_ref, acc_ref, stat_ref, out_ref):
    column = lax.broadcasted_iota(jnp.int32, (1, LIST * BLOCK), 1)
    entry = (column % (LIST * SHARE)) // SHARE
    for e in range(KEY_HEADS):
        k = far_ref[:, 2 * e * WIDTH : (2 * e + 1) * WIDTH]
        v = far_ref[:, (2 * e + 1) * WIDTH : (2 * e + 2) * WIDTH]
        mask = entry < live_ref[e]
        q = jnp.concatenate(
            [
                q_ref[:, (e * GROUP + h) * WIDTH : (e * GROUP + h + 1) * WIDTH]
                for h in range(GROUP)
            ],
            axis=0,
        )
        s = lax.dot_general(q, k, (((1,), (1,)), ((), ())), preferred_element_type=jnp.float32)
        s = jnp.where(mask, s, -1e30)
        near_top = stat_ref[e, :, 0:1]
        near_total = stat_ref[e, :, 1:2]
        top = jnp.maximum(near_top, jnp.max(s, axis=1, keepdims=True))
        w = jnp.exp2((s - top) * SCALE_LOG2)
        back = jnp.exp2((near_top - top) * SCALE_LOG2)
        total = back * near_total + jnp.sum(w, axis=1, keepdims=True)
        acc = back * acc_ref[e] + jnp.dot(
            w.astype(jnp.bfloat16), v, preferred_element_type=jnp.float32
        )
        res = (acc / total).astype(jnp.bfloat16)
        for h in range(GROUP):
            head = slice((e * GROUP + h) * WIDTH, (e * GROUP + h + 1) * WIDTH)
            out_ref[:, head] = res[h * BLOCK : (h + 1) * BLOCK]


def far_attention(live, queries, far, acc, stat):
    vmem = pl.BlockSpec(memory_space=pltpu.VMEM)
    return pl.pallas_call(
        far_kernel,
        in_specs=[pl.BlockSpec(memory_space=pltpu.SMEM), vmem, vmem, vmem, vmem],
        out_specs=vmem,
        out_shape=jax.ShapeDtypeStruct((BLOCK, KEY_HEADS * GROUP * WIDTH), jnp.bfloat16),
        compiler_params=pltpu.CompilerParams(vmem_limit_bytes=16 * MIB),
        name="far",
    )(live, queries, far, acc, stat)


def pick_kernel(index_ref, main_ref, rest_ref, out_ref):
    lane = lax.broadcasted_iota(jnp.int32, (PICKED, UNIT * ZH), 1)
    for e in range(KEY_HEADS):
        hot = jnp.where(lane == index_ref[:, e : e + 1], 1.0, 0.0).astype(jnp.bfloat16)
        source = slice(2 * WIDTH * (e % 2), 2 * WIDTH * (e % 2 + 1))
        table = jnp.concatenate([main_ref[:, source], rest_ref[:, source]], axis=0)
        out_ref[:, 2 * WIDTH * e : 2 * WIDTH * (e + 1)] = jnp.dot(
            hot, table, preferred_element_type=jnp.float32
        ).astype(jnp.bfloat16)


def pick(index, main, rest):
    return pl.pallas_call(
        pick_kernel,
        out_shape=jax.ShapeDtypeStruct((PICKED, LANES), jnp.bfloat16),
        compiler_params=pltpu.CompilerParams(vmem_limit_bytes=16 * MIB),
        name="pick",
    )(index, main, rest)


def local(queries, keys, values, far_blocks, far_live_length):
    odd = lax.axis_index("x") % 2
    both = jnp.stack(
        [keys.reshape(KDEV, KEY_HEADS, WIDTH), values.reshape(KDEV, KEY_HEADS, WIDTH)], axis=2
    ).reshape(KDEV, LANES)
    near = lax.all_gather(both, ("y", "x"), axis=0, tiled=True)

    low, high = both[:, :HALF], both[:, HALF:]
    pairs = jnp.stack([jnp.where(odd, high, low), jnp.where(odd, low, high)], axis=0)
    pairs = pairs.reshape(2, PEERS // 2, SHARE, HALF).transpose(1, 0, 2, 3)
    pairs = pairs.reshape(PEERS, SHARE, HALF)
    ids = far_blocks.reshape(1, 1, KEY_HEADS * LIST).astype(jnp.bfloat16)
    ids = jnp.pad(ids, ((0, 0), (0, 0), (0, WIDTH - KEY_HEADS * LIST)))
    ids = jnp.broadcast_to(ids, (PEERS, SHARE, WIDTH))
    got = lax.all_to_all(
        jnp.concatenate([pairs, ids], axis=2), PEER_AXES, 0, 0, tiled=True
    )
    unit = got[:, :, :HALF].reshape(UNIT, HALF)
    asked = got[:, 0, HALF : HALF + KEY_HEADS * LIST].astype(jnp.int32)

    rest = jnp.broadcast_to(unit[None, MAIN:], (ZH, REST, HALF)).reshape(ZH * REST, HALF)
    rest = lax.all_to_all(rest, "zh", 0, 0, tiled=True)
    main = lax.all_gather(unit[:MAIN], "zh", axis=0, tiled=True)

    asked = asked.reshape(PEERS, KEY_HEADS, LIST, 1)
    head_pair = jnp.arange(KEY_HEADS, dtype=jnp.int32).reshape(KEY_HEADS, 1, 1) // 2
    row = ((asked % BLOCKS_PAIR) * 2 + (head_pair ^ odd)) * SHARE
    row = row + jnp.arange(SHARE, dtype=jnp.int32)
    place = asked // BLOCKS_PAIR
    row = jnp.where(row < MAIN, place * MAIN + row, ZH * MAIN + place * REST + row - MAIN)
    index = row.transpose(0, 2, 3, 1).reshape(PICKED, KEY_HEADS)

    picked = pick(index, main, rest)
    picked, queries, near = lax.optimization_barrier((picked, queries, near))
    arrived = lax.all_to_all(
        picked.reshape(PEERS, LIST * SHARE, LANES), PEER_AXES, 0, 0, tiled=True
    )
    acc, stat = near_attention(queries, near)
    live = far_live_length.reshape(KEY_HEADS)
    return far_attention(live, queries, arrived.reshape(LIST * BLOCK, LANES), acc, stat)


def solution(mesh):
    axes = ("zh", "zl", "c", "y", "x")
    fine = Mesh(mesh.devices.reshape(ZH, ZL, C, Y, X), axes)
    placed = (
        P(axes, None),
        P(axes, None),
        P(axes, None),
        P(axes, None, None),
        P(axes, None),
    )
    return jax.shard_map(
        local, mesh=fine, in_specs=placed, out_specs=P(axes, None), check_vma=False
    )
```

time: 141 us -> 125 us (0.89)
  starting transfers between devices: 64.9 us -> 33.5 us
  blocking collectives: 17.3 us -> 34.2 us
  Pallas kernels: 20.9 us -> 16.6 us
  other arithmetic: 0.63 us -> 3.09 us
    ppermute x15 -> x0, starting transfers between devices: 52.6 us -> none  [the longest x7 36.9 us: local(): downs.append(lax.ppermute(downs[-1], 'z', down))]
    all_gather x0 -> x1, blocking collectives: none -> 34.2 us  [local(): main = lax.all_gather(unit[:MAIN], 'zh', axis=0, tiled=True)]
    all_to_all x1 -> x3, starting transfers between devices: 12.3 us -> 33.5 us  [the longest x1 13.2 us: local(): rest = lax.all_to_all(rest, 'zh', 0, 0, tiled=True)]
    all_to_all x1 -> x0, blocking collectives: 17.3 us -> none  [local(): got = lax.all_to_all(sent, ('c', 'y', 'x'), 0, 0, tiled=True)]
    ppermute x15 -> x0, waiting for transfers between devices: 10 us -> none  [the longest x8 10 us: local(): ups.append(lax.ppermute(ups[-1], 'z', up))]
    all_to_all x1 -> x3, waiting for transfers between devices: 5.42 us -> 14.9 us  [the longest x1 8.59 us: local(): lax.all_to_all(jnp.concatenate([pairs, ids], axis=2), PEER_AXES, 0, 0, ti...]
    pallas_call x2, Pallas kernels: 12.5 us -> 9.05 us  [the longest x1 6.73 us: far_attention(): pl.pallas_call(far_kernel, in_specs=[pl.BlockSpec(memory_space=pltpu.SMEM...]
    unnamed x13 -> x11, local copies, waits for them, and re-layouts: 4.06 us -> 4.05 us
  transfers between devices with their start and end apart: 17 -> 4, of which waited for: 9 -> 2; matrix products, arithmetic and copies ran while one was open for 1% -> 4% of each run, Pallas kernels for 8% -> 8%
where the time goes in v2:
time: 125 us; the launch traced here: 124 us
  blocking collectives  34.2 us (27%)
  starting transfers between devices  33.5 us (27%)
  Pallas kernels  16.6 us (13%)
  waiting for transfers between devices  14.9 us (12%)
  between operations  13.6 us (11%)
  local copies, waits for them, and re-layouts  8.41 us (7%)
  other arithmetic  3.09 us (2%)
    all_gather x1, blocking collectives, local(): main = lax.all_gather(unit[:MAIN], 'zh', axis=0, tiled=True)  34.2 us
    all_to_all x1, starting transfers between devices, local(): rest = lax.all_to_all(rest, 'zh', 0, 0, tiled=True)  13.2 us
    all_to_all x1, starting transfers between devices, local(): lax.all_to_all(jnp.concatenate([pairs, ids], axis=2), PEER_AXES, 0, 0, ti...  11 us
    all_to_all x1, starting transfers between devices, local(): lax.all_to_all(picked.reshape(PEERS, LIST * SHARE, LANES), PEER_AXES, 0,...  9.28 us
    all_to_all x1, waiting for transfers between devices, local(): lax.all_to_all(jnp.concatenate([pairs, ids], axis=2), PEER_AXES, 0, 0, ti...  8.59 us
    pallas_call x1, Pallas kernels, near_attention(): pl.pallas_call(near_kernel, grid=(KEY_HEADS,), in_specs=[pl.BlockSpec((BL...  7.6 us
    pallas_call x1, Pallas kernels, far_attention(): pl.pallas_call(far_kernel, in_specs=[pl.BlockSpec(memory_space=pltpu.SMEM...  6.73 us
    all_to_all x1, waiting for transfers between devices, local(): lax.all_to_all(picked.reshape(PEERS, LIST * SHARE, LANES), PEER_AXES, 0,...  6.27 us
  transfers between devices with their start and end apart: 4, of which 2 were waited for; matrix products, arithmetic and copies ran while one was open for 4% of the time, Pallas kernels for 8%

profile of v2, /device:TPU:1, one launch (start us, length us, event | category | flops | bytes accessed | tf_op | source)
XLA Modules:
  0.0 124.4 jit_solution(7927311490421387215)
XLA Ops:
  6.5 0.9 stack_reshape.8
  7.4 0.9 stack_reshape.9
  8.3 0.3 pad_maximum_fusion.1
  8.6 0.7 reshape.196
  9.4 0.7 convert_element_type.52
  10.1 0.1 convert_element_type.53
  10.2 0.9 broadcast_select_fusion.1
  11.2 0.2 pad_maximum_fusion.2
  11.3 0.8 pad_maximum_fusion
  12.2 11.0 %all-to-all-start = ((bf16[64,2,640]{2,1,0:T(2,128)(2,1)}), bf16[64,2,640]{2,1,0:T(2,128)(2,1)S(1)}, u32[]{:S(2)}, u32[]{:S(2)}) async-start(bf16[64,2,640]{2,1,0:T(2,128)(2,1)} %pad_maximum_fusion), calls=%async_computation | async-start | bytes 327680 | tf_op jit(solution)/shard_map/all_to_all | solution.py:155
  23.2 0.2 add.119
  23.4 8.6 %all-to-all-done = bf16[64,2,640]{2,1,0:T(2,128)(2,1)S(1)} async-done(((bf16[64,2,640]{2,1,0:T(2,128)(2,1)}), bf16[64,2,640]{2,1,0:T(2,128)(2,1)S(1)}, u32[]{:S(2)}, u32[]{:S(2)}) %all-to-all-start) | async-done | bytes 163872 | tf_op jit(solution)/shard_map/all_to_all | solution.py:155
  32.1 0.1 copy.46
  32.1 0.7 broadcast_in_dim.20
  32.8 13.2 %all-to-all-start.1 = ((bf16[8,16,512]{2,1,0:T(8,128)(2,1)}), bf16[8,16,512]{2,1,0:T(8,128)(2,1)S(1)}, u32[]{:S(2)}, u32[]{:S(2)}) async-start(bf16[8,16,512]{2,1,0:T(8,128)(2,1)} %broadcast_in_dim.20), calls=%async_computation.1 | async-start | bytes 262144 | tf_op jit(solution)/shard_map/all_to_all | solution.py:162
  46.1 0.1 copy.43
  46.2 0.1 copy.45
  46.4 0.1 copy.44
  46.5 0.1 add.116
  46.6 0.1 add.129
  46.7 0.1 add.123
  46.8 0.1 add_select_fusion.index_ref
  47.0 0.1 slice.31
  47.1 34.2 %all_gather.6.main_ref = bf16[896,512]{1,0:T(8,128)(2,1)S(1)} all-gather(bf16[112,512]{1,0:T(8,128)(2,1)S(1)} %slice.26), channel_id=1, replica_groups=mesh['zh'=8,'zl'=2,'c'=2,'y'=4,'x'=4] {'zh'}, dimensions={0}, use_global_device_ids=true | all-gather | bytes 1032192 | tf_op jit(solution)/shard_map/all_gather | solution.py:163
  81.3 2.3 %pick.1 = bf16[512,1024]{1,0:T(8,128)(2,1)} custom-call(s32[512,4]{1,0:T(8,128)S(1)} %add_select_fusion.index_ref, bf16[896,512]{1,0:T(8,128)(2,1)S(1)} %all_gather.6.main_ref, bf16[128,512]{1,0:T(8,128)(2,1)S(1)} %bitcast.23), custom_call_target="tpu_custom_call" | custom-call | tf_op jit(solution)/shard_map/pick/pallas_call | solution.py:133
  83.7 9.3 %all-to-all-start.2 = ((bf16[64,8,1024]{2,1,0:T(8,128)(2,1)}), bf16[64,8,1024]{2,1,0:T(8,128)(2,1)S(1)}, u32[]{:S(2)}, u32[]{:S(2)}) async-start(bf16[64,8,1024]{2,1,0:T(8,128)(2,1)} %bitcast.15), calls=%async_computation.2 | async-start | bytes 2097152 | tf_op jit(solution)/shard_map/all_to_all | solution.py:175
  93.0 1.6 %copy-done.4 = bf16[1024,1024]{1,0:T(8,128)(2,1)S(1)} copy-done((bf16[1024,1024]{1,0:T(8,128)(2,1)S(1)}, bf16[1024,1024]{1,0:T(8,128)(2,1)}, u32[]{:S(2)}) %copy-start.4) | copy-done | bytes 2097176
  94.5 7.6 %near.1 = (f32[4,640,128]{2,1,0:T(8,128)S(1)}, f32[4,640,128]{2,1,0:T(8,128)S(1)}) custom-call(bf16[128,2560]{1,0:T(8,128)(2,1)S(1)} %copy-done.2, bf16[1024,1024]{1,0:T(8,128)(2,1)S(1)} %copy-done.4, bf16[1024,1024]{1,0:T(8,128)(2,1)S(1)} %copy-done.4), custom_call_target="tpu_custom_call" | custom-call | flops 1342177280 | bytes 8388608 | tf_op jit(solution)/shard_map/near/pallas_call | solution.py:52
  102.2 1.1 copy-done
  103.2 6.3 %all-to-all-done.2 = bf16[64,8,1024]{2,1,0:T(8,128)(2,1)S(1)} async-done(((bf16[64,8,1024]{2,1,0:T(8,128)(2,1)}), bf16[64,8,1024]{2,1,0:T(8,128)(2,1)S(1)}, u32[]{:S(2)}, u32[]{:S(2)}) %all-to-all-start.2) | async-done | bytes 1048608 | tf_op jit(solution)/shard_map/all_to_all | solution.py:175
  109.5 1.3 %copy-done.1 = f32[4,640,128]{2,1,0:T(8,128)S(1)} copy-done((f32[4,640,128]{2,1,0:T(8,128)S(1)}, f32[4,640,128]{2,1,0:T(8,128)}, u32[]{:S(2)}) %copy-start.1) | copy-done | bytes 1310744
  110.8 6.7 %far.1 = bf16[128,2560]{1,0:T(8,128)(2,1)} custom-call(s32[4]{0:T(128)S(1)} %bitcast.24, bf16[128,2560]{1,0:T(8,128)(2,1)S(1)} %copy-done.2, bf16[512,1024]{1,0:T(8,128)(2,1)S(1)} %bitcast.22, f32[4,640,128]{2,1,0:T(8,128)S(1)} %get-tuple-element.13.acc_ref, f32[4,640,128]{2,1,0:T(8,128)S(1)} %copy-done.1), custom_call_target="tpu_custom_call" | custom-call | tf_op jit(solution)/shard_map/far/pallas_call | solution.py:111
  (22 shorter events, 0.3 us)
Async XLA Ops:
  6.5 77.1 %all-gather.2.cloned.1.call-start = ((), (), s32[]{:S(2)}) async-start(), calls=%async_computation.3 | async-start | bytes 2228224 | tf_op jit(solution)/shard_map/all_gather | solution.py:146
  12.2 19.8 %all-to-all-start = ((bf16[64,2,640]{2,1,0:T(2,128)(2,1)}), bf16[64,2,640]{2,1,0:T(2,128)(2,1)S(1)}, u32[]{:S(2)}, u32[]{:S(2)}) async-start(bf16[64,2,640]{2,1,0:T(2,128)(2,1)} %pad_maximum_fusion), calls=%async_computation | async-start | bytes 327680 | tf_op jit(solution)/shard_map/all_to_all | solution.py:155
  32.8 48.5 %all-to-all-start.1 = ((bf16[8,16,512]{2,1,0:T(8,128)(2,1)}), bf16[8,16,512]{2,1,0:T(8,128)(2,1)S(1)}, u32[]{:S(2)}, u32[]{:S(2)}) async-start(bf16[8,16,512]{2,1,0:T(8,128)(2,1)} %broadcast_in_dim.20), calls=%async_computation.1 | async-start | bytes 262144 | tf_op jit(solution)/shard_map/all_to_all | solution.py:162
  83.7 9.3 %copy-start.2 = (bf16[128,2560]{1,0:T(8,128)(2,1)S(1)}, bf16[128,2560]{1,0:T(8,128)(2,1)}, u32[]{:S(2)}) copy-start(bf16[128,2560]{1,0:T(8,128)(2,1)} %q_ref.1) | copy-start | bytes 1966084
  83.7 25.8 %all-to-all-start.2 = ((bf16[64,8,1024]{2,1,0:T(8,128)(2,1)}), bf16[64,8,1024]{2,1,0:T(8,128)(2,1)S(1)}, u32[]{:S(2)}, u32[]{:S(2)}) async-start(bf16[64,8,1024]{2,1,0:T(8,128)(2,1)} %bitcast.15), calls=%async_computation.2 | async-start | bytes 2097152 | tf_op jit(solution)/shard_map/all_to_all | solution.py:175
  93.0 1.6 %copy-start.4 = (bf16[1024,1024]{1,0:T(8,128)(2,1)S(1)}, bf16[1024,1024]{1,0:T(8,128)(2,1)}, u32[]{:S(2)}) copy-start(bf16[1024,1024]{1,0:T(8,128)(2,1)} %all-gather.2.cloned.1.call-done.k_ref.v_ref) | copy-start | bytes 6291460
  94.5 14.9 %copy-start.3 = (s32[1,4]{1,0:T(1,128)S(1)}, s32[1,4]{1,0:T(1,128)}, u32[]{:S(2)}) copy-start(s32[1,4]{1,0:T(1,128)} %param.9) | copy-start | bytes 52
  102.2 1.1 copy-start
  109.5 1.3 %copy-start.1 = (f32[4,640,128]{2,1,0:T(8,128)S(1)}, f32[4,640,128]{2,1,0:T(8,128)}, u32[]{:S(2)}) copy-start(f32[4,640,128]{2,1,0:T(8,128)} %copy-done) | copy-start | bytes 3932164
Sparse Core Ops, SparseCore 0:
  10.4 64.6 all-gather.1

commit v3 on v2

v3 whole, which is shorter than its diff:
```python
import functools
import math

import jax
import jax.numpy as jnp
from jax import lax
from jax.experimental import pallas as pl
from jax.experimental.pallas import tpu as pltpu
from jax.sharding import Mesh, PartitionSpec as P

KEY_HEADS = 4
GROUP = 5
WIDTH = 128
BLOCK = 128
LIST = 4
ZH, ZL, C, Y, X = 4, 4, 2, 4, 4
PEERS = ZL * C * Y * X
PEER_AXES = ("zl", "c", "y", "x")
KDEV = 64
NEAR = Y * X * KDEV
LANES = KEY_HEADS * 2 * WIDTH
PAIR = LANES // 2
TILES = PAIR // WIDTH
CHUNK = 8
SHARE = 2
PICKED = PEERS * LIST * SHARE
SCALE_LOG2 = math.log2(math.e) / math.sqrt(WIDTH)
MIB = 1024 * 1024
QROWS = GROUP * BLOCK


def stack_heads(q_ref):
    return jnp.concatenate([q_ref[:, h * WIDTH : (h + 1) * WIDTH] for h in range(GROUP)], axis=0)


def weigh(s, top):
    tiles = [
        jnp.exp2((s[:, k * WIDTH : (k + 1) * WIDTH] - top) * SCALE_LOG2)
        for k in range(s.shape[1] // WIDTH)
    ]
    return jnp.concatenate(tiles, axis=1).astype(jnp.bfloat16)


def row_top(s):
    top = s[:, :WIDTH]
    for k in range(1, s.shape[1] // WIDTH):
        top = jnp.maximum(top, s[:, k * WIDTH : (k + 1) * WIDTH])
    return jnp.broadcast_to(jnp.max(top, axis=1, keepdims=True), top.shape)


def weighted(w, v):
    ones = jnp.ones((v.shape[0], WIDTH), jnp.bfloat16)
    return jnp.dot(w, jnp.concatenate([v, ones], axis=1), preferred_element_type=jnp.float32)


def scores(q, k):
    return lax.dot_general(q, k, (((1,), (1,)), ((), ())), preferred_element_type=jnp.float32)


def diagonal():
    shape = (BLOCK, WIDTH)
    return lax.broadcasted_iota(jnp.int32, shape, 0) == lax.broadcasted_iota(jnp.int32, shape, 1)


def near_kernel(q_ref, k_ref, v_ref, mean_ref, log_ref):
    s = scores(stack_heads(q_ref), k_ref[...])
    top = row_top(s)
    both = weighted(weigh(s, top), v_ref[...])
    total = both[:, WIDTH:]
    mean_ref[0] = both[:, :WIDTH] / total
    log_ref[0] = jnp.zeros((8, WIDTH), jnp.float32)
    log = top + jnp.log2(total) * (1.0 / SCALE_LOG2)
    for h in range(GROUP):
        own = jnp.where(diagonal(), log[h * BLOCK : (h + 1) * BLOCK], 0.0)
        log_ref[0, h : h + 1] = jnp.sum(own, axis=0, keepdims=True)


def near_attention(queries, near):
    return pl.pallas_call(
        near_kernel,
        grid=(KEY_HEADS,),
        in_specs=[
            pl.BlockSpec((BLOCK, GROUP * WIDTH), lambda e: (0, e)),
            pl.BlockSpec((NEAR, WIDTH), lambda e: (0, 2 * e)),
            pl.BlockSpec((NEAR, WIDTH), lambda e: (0, 2 * e + 1)),
        ],
        out_specs=[
            pl.BlockSpec((1, QROWS, WIDTH), lambda e: (e, 0, 0)),
            pl.BlockSpec((1, 8, WIDTH), lambda e: (e, 0, 0)),
        ],
        out_shape=[
            pltpu.VMEM((KEY_HEADS, QROWS, WIDTH), jnp.float32),
            pltpu.VMEM((KEY_HEADS, 8, WIDTH), jnp.float32),
        ],
        compiler_params=pltpu.CompilerParams(vmem_limit_bytes=16 * MIB),
        cost_estimate=pl.CostEstimate(
            flops=200 * KEY_HEADS * QROWS * NEAR * WIDTH,
            bytes_accessed=8 * MIB,
            transcendentals=KEY_HEADS * QROWS * NEAR,
        ),
        name="near",
    )(
        pltpu.with_memory_space_constraint(queries, pltpu.HBM),
        pltpu.with_memory_space_constraint(near, pltpu.HBM),
        pltpu.with_memory_space_constraint(near, pltpu.HBM),
    )


def far_kernel(live_ref, q_ref, far_ref, mean_ref, log_ref, out_ref):
    column = lax.broadcasted_iota(jnp.int32, (1, LIST * BLOCK), 1)
    entry = (column % (LIST * SHARE)) // SHARE
    for e in range(KEY_HEADS):
        rows = slice(e // 2 * LIST * BLOCK, (e // 2 + 1) * LIST * BLOCK)
        k = far_ref[rows, 2 * (e % 2) * WIDTH : (2 * (e % 2) + 1) * WIDTH]
        v = far_ref[rows, (2 * (e % 2) + 1) * WIDTH : (2 * (e % 2) + 2) * WIDTH]
        q = stack_heads(q_ref.at[:, e * GROUP * WIDTH : (e + 1) * GROUP * WIDTH])
        s = jnp.where(entry < live_ref[e], scores(q, k), -1e30)
        near_log = jnp.concatenate(
            [
                jnp.broadcast_to(
                    jnp.sum(
                        jnp.where(diagonal(), log_ref[e, h : h + 1], 0.0), axis=1, keepdims=True
                    ),
                    (BLOCK, WIDTH),
                )
                for h in range(GROUP)
            ],
            axis=0,
        )
        top = jnp.maximum(near_log, row_top(s))
        back = jnp.exp2((near_log - top) * SCALE_LOG2)
        both = weighted(weigh(s, top), v)
        acc = back * mean_ref[e] + both[:, :WIDTH]
        total = back + both[:, WIDTH:]
        res = (acc / total).astype(jnp.bfloat16)
        for h in range(GROUP):
            head = slice((e * GROUP + h) * WIDTH, (e * GROUP + h + 1) * WIDTH)
            out_ref[:, head] = res[h * BLOCK : (h + 1) * BLOCK]


def far_attention(live, queries, far, mean, log):
    vmem = pl.BlockSpec(memory_space=pltpu.VMEM)
    return pl.pallas_call(
        far_kernel,
        in_specs=[pl.BlockSpec(memory_space=pltpu.SMEM), vmem, vmem, vmem, vmem],
        out_specs=vmem,
        out_shape=jax.ShapeDtypeStruct((BLOCK, KEY_HEADS * GROUP * WIDTH), jnp.bfloat16),
        compiler_params=pltpu.CompilerParams(vmem_limit_bytes=16 * MIB),
        name="far",
    )(
        live,
        queries,
        far,
        pltpu.with_memory_space_constraint(mean, pltpu.VMEM),
        pltpu.with_memory_space_constraint(log, pltpu.VMEM),
    )


def prep_kernel(ids_ref, k_ref, v_ref, near_ref, sent_ref):
    tiles = []
    for e in range(KEY_HEADS):
        tiles.append(k_ref[:, e * WIDTH : (e + 1) * WIDTH])
        tiles.append(v_ref[:, e * WIDTH : (e + 1) * WIDTH])
    near_ref[...] = jnp.concatenate(tiles, axis=1)
    shape = (KDEV * CHUNK, KDEV * TILES)
    row = lax.broadcasted_iota(jnp.int32, shape, 0)
    column = lax.broadcasted_iota(jnp.int32, shape, 1)
    target = jnp.where(row % CHUNK < TILES, row % CHUNK * KDEV + row // CHUNK, -1)
    hot = jnp.where(column == target, 1.0, 0.0).astype(jnp.bfloat16)
    shape = (KDEV * CHUNK, WIDTH)
    lane = lax.broadcasted_iota(jnp.int32, shape, 1)
    is_id = lax.broadcasted_iota(jnp.int32, shape, 0) % CHUNK >= TILES
    ids = jnp.zeros(shape, jnp.float32)
    for i in range(KEY_HEADS * LIST):
        ids = jnp.where(lane == i, ids_ref[i].astype(jnp.float32), ids)
    for j in range(2):
        moved = jnp.dot(
            hot,
            jnp.concatenate(tiles[j * TILES : (j + 1) * TILES], axis=0),
            preferred_element_type=jnp.float32,
        )
        rows = slice(j * KDEV * CHUNK, (j + 1) * KDEV * CHUNK)
        sent_ref[rows] = jnp.where(is_id, ids, moved).astype(jnp.bfloat16)


def prep(ids, keys, values):
    whole = lambda shape: pl.BlockSpec(shape, lambda i: (0, 0))
    return pl.pallas_call(
        prep_kernel,
        grid=(1,),
        in_specs=[
            pl.BlockSpec(memory_space=pltpu.SMEM),
            whole((KDEV, LANES // 2)),
            whole((KDEV, LANES // 2)),
        ],
        out_specs=[whole((KDEV, LANES)), whole((PEERS * CHUNK, WIDTH))],
        out_shape=[
            jax.ShapeDtypeStruct((KDEV, LANES), jnp.bfloat16),
            jax.ShapeDtypeStruct((PEERS * CHUNK, WIDTH), jnp.bfloat16),
        ],
        compiler_params=pltpu.CompilerParams(vmem_limit_bytes=16 * MIB),
        name="prep",
    )(
        ids,
        pltpu.with_memory_space_constraint(keys, pltpu.HBM),
        pltpu.with_memory_space_constraint(values, pltpu.HBM),
    )


def pick_kernel(index_ref, table_ref, out_ref):
    lane = lax.broadcasted_iota(jnp.int32, (PICKED, PEERS * ZH), 1)
    for e in range(2):
        hot = jnp.where(lane == index_ref[:, e : e + 1], 1.0, 0.0).astype(jnp.bfloat16)
        lanes = slice(2 * WIDTH * e, 2 * WIDTH * (e + 1))
        out_ref[:, lanes] = jnp.dot(
            hot, table_ref[:, lanes], preferred_element_type=jnp.float32
        ).astype(jnp.bfloat16)


def pick(index, table):
    return pl.pallas_call(
        pick_kernel,
        out_shape=jax.ShapeDtypeStruct((PICKED, PAIR), jnp.bfloat16),
        compiler_params=pltpu.CompilerParams(vmem_limit_bytes=16 * MIB),
        name="pick",
    )(index, table)


def local(queries, keys, values, far_blocks, far_live_length):
    near, sent = prep(far_blocks.reshape(KEY_HEADS * LIST), keys, values)
    near = lax.all_gather(near, ("y", "x"), axis=0, tiled=True)
    got = lax.all_to_all(sent.reshape(PEERS, CHUNK, WIDTH), PEER_AXES, 0, 0, tiled=True)
    table = lax.all_gather(got[:, :TILES].reshape(PEERS, PAIR), "zh", axis=0, tiled=True)

    asked = got[:, TILES, : KEY_HEADS * LIST].astype(jnp.int32).reshape(PEERS, 2, 2, LIST)
    asked = jnp.where(lax.axis_index("zl") < ZL // 2, asked[:, 0], asked[:, 1])
    half = jnp.arange(SHARE, dtype=jnp.int32).reshape(1, 1, SHARE, 1)
    index = asked.transpose(0, 2, 1)[:, :, None] * SHARE + half
    picked = pick(index.reshape(PICKED, 2), table)

    picked, queries = lax.optimization_barrier((picked, queries))
    arrived = lax.all_to_all(
        picked.reshape(PEERS, LIST * SHARE, PAIR), PEER_AXES, 0, 0, tiled=True
    )
    mean, log = near_attention(queries, near)
    live = far_live_length.reshape(KEY_HEADS)
    return far_attention(live, queries, arrived.reshape(PICKED, PAIR), mean, log)


def solution(mesh):
    axes = ("zh", "zl", "c", "y", "x")
    fine = Mesh(mesh.devices.reshape(ZH, ZL, C, Y, X), axes)
    placed = (
        P(axes, None),
        P(axes, None),
        P(axes, None),
        P(axes, None, None),
        P(axes, None),
    )
    return jax.shard_map(
        local, mesh=fine, in_specs=placed, out_specs=P(axes, None), check_vma=False
    )
```

time: 125 us -> 118 us (0.944)
  waiting for transfers between devices: 14.9 us -> 34.9 us
  starting transfers between devices: 33.5 us -> 20.8 us
  local copies, waits for them, and re-layouts: 8.41 us -> 1.62 us
  other arithmetic: 3.09 us -> 0.21 us
  blocking collectives: 34.2 us -> 32.2 us
  Pallas kernels: 16.6 us -> 14.9 us
    all_to_all x3 -> x2, waiting for transfers between devices: 14.9 us -> 34.8 us  [the longest x1 21.8 us: local(): lax.all_to_all(picked.reshape(PEERS, LIST * SHARE, PAIR), PEER_AXES, 0, 0...]
    all_to_all x3 -> x2, starting transfers between devices: 33.5 us -> 20.8 us  [the longest x1 13.9 us: local(): lax.all_to_all(sent.reshape(PEERS, CHUNK, WIDTH), PEER_AXES, 0, 0, tiled=...]
    unnamed x11 -> x6, local copies, waits for them, and re-layouts: 4.05 us -> 0.12 us
    pallas_call x1, Pallas kernels: 6.73 us -> 3.57 us  [far_attention(): pl.pallas_call(far_kernel, in_specs=[pl.BlockSpec(memory_space=pltpu.SMEM...]
    all_gather x1, blocking collectives: 34.2 us -> 32.2 us  [local(): lax.all_gather(got[:, :TILES].reshape(PEERS, PAIR), 'zh', axis=0, tiled=T...]
    another operation x4 -> x0, local copies, waits for them, and re-layouts: 1.82 us -> none  [the longest x2 1.75 us: local(): jnp.stack([keys.reshape(KDEV, KEY_HEADS, WIDTH), values.reshape(KDEV, KEY...]
    pallas_call x1 -> x2, Pallas kernels: 2.31 us -> 3.75 us  [the longest x1 1.89 us: prep(): pl.pallas_call(prep_kernel, grid=(1,), in_specs=[pl.BlockSpec(memory_spac...]
  transfers between devices with their start and end apart: 4 -> 3, of which waited for: 2 -> 2; matrix products, arithmetic and copies ran while one was open for 4% -> 1% of each run, Pallas kernels for 8% -> 8%
where the time goes in v3:
time: 118 us
  waiting for transfers between devices  34.9 us (30%)
  blocking collectives  32.2 us (27%)
  starting transfers between devices  20.8 us (18%)
  Pallas kernels  14.9 us (13%)
  between operations  13.5 us (11%)
  local copies, waits for them, and re-layouts  1.62 us (1%)
    all_gather x1, blocking collectives, local(): lax.all_gather(got[:, :TILES].reshape(PEERS, PAIR), 'zh', axis=0, tiled=T...  32.2 us
    all_to_all x1, waiting for transfers between devices, local(): lax.all_to_all(picked.reshape(PEERS, LIST * SHARE, PAIR), PEER_AXES, 0, 0...  21.8 us
    all_to_all x1, starting transfers between devices, local(): lax.all_to_all(sent.reshape(PEERS, CHUNK, WIDTH), PEER_AXES, 0, 0, tiled=...  13.9 us
    all_to_all x1, waiting for transfers between devices, local(): lax.all_to_all(sent.reshape(PEERS, CHUNK, WIDTH), PEER_AXES, 0, 0, tiled=...  13.1 us
    pallas_call x1, Pallas kernels, near_attention(): pl.pallas_call(near_kernel, grid=(KEY_HEADS,), in_specs=[pl.BlockSpec((BL...  7.54 us
    all_to_all x1, starting transfers between devices, local(): lax.all_to_all(picked.reshape(PEERS, LIST * SHARE, PAIR), PEER_AXES, 0, 0...  6.95 us
    pallas_call x1, Pallas kernels, far_attention(): pl.pallas_call(far_kernel, in_specs=[pl.BlockSpec(memory_space=pltpu.SMEM...  3.57 us
  transfers between devices with their start and end apart: 3, of which 2 were waited for; matrix products, arithmetic and copies ran while one was open for 1% of the time, Pallas kernels for 8%

profile of v3, /device:TPU:1, one launch (start us, length us, event | category | flops | bytes accessed | tf_op | source)
XLA Modules:
  0.0 118.0 jit_solution(1052647126495057442)
XLA Ops:
  6.5 0.0 all-gather.2.cloned.1.call-start
  6.5 0.8 reshape.33.ids_ref
  7.3 1.9 %prep.1 = (bf16[64,1024]{1,0:T(8,128)(2,1)}, bf16[1024,128]{1,0:T(8,128)(2,1)}) custom-call(s32[16]{0:T(128)S(1)} %reshape.33.ids_ref, bf16[64,512]{1,0:T(8,128)(2,1)} %k_ref.1, bf16[64,512]{1,0:T(8,128)(2,1)} %v_ref.1), custom_call_target="tpu_custom_call" | custom-call | tf_op jit(solution)/shard_map/prep/pallas_call | solution.py:188
  9.2 0.0 all-gather.2.cloned.1.call-update
  9.2 13.9 %all-to-all-start = ((bf16[128,8,128]{2,1,0:T(8,128)(2,1)}), bf16[128,8,128]{2,1,0:T(8,128)(2,1)S(1)}, u32[]{:S(2)}, u32[]{:S(2)}) async-start(bf16[128,8,128]{2,1,0:T(8,128)(2,1)} %bitcast.1), calls=%async_computation | async-start | bytes 524288 | tf_op jit(solution)/shard_map/all_to_all | solution.py:232
  23.1 0.2 add.23
  23.4 13.1 %all-to-all-done = bf16[128,8,128]{2,1,0:T(8,128)(2,1)S(1)} async-done(((bf16[128,8,128]{2,1,0:T(8,128)(2,1)}), bf16[128,8,128]{2,1,0:T(8,128)(2,1)S(1)}, u32[]{:S(2)}, u32[]{:S(2)}) %all-to-all-start) | async-done | bytes 262176 | tf_op jit(solution)/shard_map/all_to_all | solution.py:232
  36.4 0.1 slice.16
  36.5 0.1 copy.12
  36.6 0.2 copy.11
  36.9 32.2 %all_gather.6.table_ref = bf16[512,512]{1,0:T(8,128)(2,1)S(1)} all-gather(bf16[128,512]{1,0:T(8,128)(2,1)S(1)} %bitcast.18), channel_id=1, replica_groups=mesh['zh'=4,'zl'=4,'c'=2,'y'=4,'x'=4] {'zh'}, dimensions={0}, use_global_device_ids=true | all-gather | bytes 655360 | tf_op jit(solution)/shard_map/all_gather | solution.py:233
  69.0 0.2 add.20
  69.2 0.2 broadcast_add_fusion.index_ref
  69.4 1.9 %pick.1 = bf16[1024,512]{1,0:T(8,128)(2,1)} custom-call(s32[1024,2]{1,0:T(8,128)S(1)} %broadcast_add_fusion.index_ref, bf16[512,512]{1,0:T(8,128)(2,1)S(1)} %all_gather.6.table_ref), custom_call_target="tpu_custom_call" | custom-call | tf_op jit(solution)/shard_map/pick/pallas_call | solution.py:221
  71.3 6.9 %all-to-all-start.1 = ((bf16[128,8,512]{2,1,0:T(8,128)(2,1)}), bf16[128,8,512]{2,1,0:T(8,128)(2,1)S(1)}, u32[]{:S(2)}, u32[]{:S(2)}) async-start(bf16[128,8,512]{2,1,0:T(8,128)(2,1)} %bitcast.7), calls=%async_computation.1 | async-start | bytes 2097152 | tf_op jit(solution)/shard_map/all_to_all | solution.py:242
  78.2 0.0 copy-start
  78.3 0.0 copy-start.1
  78.3 0.0 all-gather.2.cloned.1.call-done.k_ref.v_ref
  78.3 7.5 %near.1 = (f32[4,640,128]{2,1,0:T(8,128)S(1)}, f32[4,8,128]{2,1,0:T(8,128)S(1)}) custom-call(bf16[128,2560]{1,0:T(8,128)(2,1)} %q_ref.1, bf16[1024,1024]{1,0:T(8,128)(2,1)} %all-gather.2.cloned.1.call-done.k_ref.v_ref, bf16[1024,1024]{1,0:T(8,128)(2,1)} %all-gather.2.cloned.1.call-done.k_ref.v_ref), custom_call_target="tpu_custom_call" | custom-call | flops 67108864000 | bytes 8388608 | tf_op jit(solution)/shard_map/near/pallas_call | solution.py:79
  85.8 21.8 %all-to-all-done.1 = bf16[128,8,512]{2,1,0:T(8,128)(2,1)S(1)} async-done(((bf16[128,8,512]{2,1,0:T(8,128)(2,1)}), bf16[128,8,512]{2,1,0:T(8,128)(2,1)S(1)}, u32[]{:S(2)}, u32[]{:S(2)}) %all-to-all-start.1) | async-done | bytes 1048608 | tf_op jit(solution)/shard_map/all_to_all | solution.py:242
  107.6 0.0 copy-done
  107.6 0.0 copy-done.1
  107.6 3.6 %far.1 = bf16[128,2560]{1,0:T(8,128)(2,1)} custom-call(s32[4]{0:T(128)S(1)} %bitcast.16, bf16[128,2560]{1,0:T(8,128)(2,1)S(1)} %copy-done, bf16[1024,512]{1,0:T(8,128)(2,1)S(1)} %bitcast.15, f32[4,640,128]{2,1,0:T(8,128)S(1)} %get-tuple-element.15.mean_ref, f32[4,8,128]{2,1,0:T(8,128)S(1)} %get-tuple-element.16.log_ref), custom_call_target="tpu_custom_call" | custom-call | tf_op jit(solution)/shard_map/far/pallas_call | solution.py:143
  (5 shorter events, 0.1 us)
Async XLA Ops:
  6.5 71.8 %all-gather.2.cloned.1.call-start = ((), (), s32[]{:S(2)}) async-start(), calls=%async_computation.2 | async-start | bytes 2228224 | tf_op jit(solution)/shard_map/all_gather | solution.py:231
  9.2 27.2 %all-to-all-start = ((bf16[128,8,128]{2,1,0:T(8,128)(2,1)}), bf16[128,8,128]{2,1,0:T(8,128)(2,1)S(1)}, u32[]{:S(2)}, u32[]{:S(2)}) async-start(bf16[128,8,128]{2,1,0:T(8,128)(2,1)} %bitcast.1), calls=%async_computation | async-start | bytes 524288 | tf_op jit(solution)/shard_map/all_to_all | solution.py:232
  71.3 36.3 %all-to-all-start.1 = ((bf16[128,8,512]{2,1,0:T(8,128)(2,1)}), bf16[128,8,512]{2,1,0:T(8,128)(2,1)S(1)}, u32[]{:S(2)}, u32[]{:S(2)}) async-start(bf16[128,8,512]{2,1,0:T(8,128)(2,1)} %bitcast.7), calls=%async_computation.1 | async-start | bytes 2097152 | tf_op jit(solution)/shard_map/all_to_all | solution.py:242
  78.2 29.4 %copy-start = (bf16[128,2560]{1,0:T(8,128)(2,1)S(1)}, bf16[128,2560]{1,0:T(8,128)(2,1)}, u32[]{:S(2)}) copy-start(bf16[128,2560]{1,0:T(8,128)(2,1)} %q_ref.1) | copy-start | bytes 1966084
  78.3 29.4 %copy-start.1 = (s32[1,4]{1,0:T(1,128)S(1)}, s32[1,4]{1,0:T(1,128)}, u32[]{:S(2)}) copy-start(s32[1,4]{1,0:T(1,128)} %param.9) | copy-start | bytes 52
Sparse Core Ops, SparseCore 0:
  10.4 64.6 all-gather.1

commit v4 on v3

--- a/solution.py
+++ b/solution.py
@@ -21,6 +21,7 @@
 LANES = KEY_HEADS * 2 * WIDTH
 PAIR = LANES // 2
 TILES = PAIR // WIDTH
+COPIES = Y * X
 CHUNK = 8
 SHARE = 2
 PICKED = PEERS * LIST * SHARE
@@ -161,7 +162,9 @@
     for e in range(KEY_HEADS):
         tiles.append(k_ref[:, e * WIDTH : (e + 1) * WIDTH])
         tiles.append(v_ref[:, e * WIDTH : (e + 1) * WIDTH])
-    near_ref[...] = jnp.concatenate(tiles, axis=1)
+    own = jnp.concatenate(tiles, axis=1)
+    for i in range(COPIES):
+        near_ref[i * KDEV : (i + 1) * KDEV] = own
     shape = (KDEV * CHUNK, KDEV * TILES)
     row = lax.broadcasted_iota(jnp.int32, shape, 0)
     column = lax.broadcasted_iota(jnp.int32, shape, 1)
@@ -193,9 +196,9 @@
             whole((KDEV, LANES // 2)),
             whole((KDEV, LANES // 2)),
         ],
-        out_specs=[whole((KDEV, LANES)), whole((PEERS * CHUNK, WIDTH))],
+        out_specs=[whole((COPIES * KDEV, LANES)), whole((PEERS * CHUNK, WIDTH))],
         out_shape=[
-            jax.ShapeDtypeStruct((KDEV, LANES), jnp.bfloat16),
+            jax.ShapeDtypeStruct((COPIES * KDEV, LANES), jnp.bfloat16),
             jax.ShapeDtypeStruct((PEERS * CHUNK, WIDTH), jnp.bfloat16),
         ],
         compiler_params=pltpu.CompilerParams(vmem_limit_bytes=16 * MIB),
@@ -228,7 +231,7 @@
 
 def local(queries, keys, values, far_blocks, far_live_length):
     near, sent = prep(far_blocks.reshape(KEY_HEADS * LIST), keys, values)
-    near = lax.all_gather(near, ("y", "x"), axis=0, tiled=True)
+    near = lax.all_to_all(near, ("y", "x"), 0, 0, tiled=True)
     got = lax.all_to_all(sent.reshape(PEERS, CHUNK, WIDTH), PEER_AXES, 0, 0, tiled=True)
     table = lax.all_gather(got[:, :TILES].reshape(PEERS, PAIR), "zh", axis=0, tiled=True)
 

time: 118 us -> 111 us (0.941)
  blocking collectives: 32.2 us -> 58.2 us
  between operations: 13.5 us -> 0.12 us
  waiting for transfers between devices: 34.9 us -> 21.8 us
  starting transfers between devices: 20.8 us -> 13.3 us
    all_to_all x0 -> x1, blocking collectives: none -> 27 us  [local(): lax.all_to_all(sent.reshape(PEERS, CHUNK, WIDTH), PEER_AXES, 0, 0, tiled=...]
    all_to_all x1, waiting for transfers between devices: 13.1 us -> 0.01 us  [local(): near = lax.all_to_all(near, ('y', 'x'), 0, 0, tiled=True)]
    all_to_all x1, starting transfers between devices: 13.9 us -> 3.72 us  [local(): near = lax.all_to_all(near, ('y', 'x'), 0, 0, tiled=True)]
    all_to_all x1, starting transfers between devices: 6.95 us -> 9.59 us  [local(): lax.all_to_all(picked.reshape(PEERS, LIST * SHARE, PAIR), PEER_AXES, 0, 0...]
  transfers between devices with their start and end apart: 3 -> 2, of which waited for: 2 -> 1; matrix products, arithmetic and copies ran while one was open for 1% -> 1% of each run, Pallas kernels for 8% -> 8%
where the time goes in v4:
time: 111 us
  blocking collectives  58.2 us (52%)
  waiting for transfers between devices  21.8 us (20%)
  Pallas kernels  15.5 us (14%)
  starting transfers between devices  13.3 us (12%)
  local copies, waits for them, and re-layouts  1.62 us (1%)
    all_gather x1, blocking collectives, local(): lax.all_gather(got[:, :TILES].reshape(PEERS, PAIR), 'zh', axis=0, tiled=T...  31.3 us
    all_to_all x1, blocking collectives, local(): lax.all_to_all(sent.reshape(PEERS, CHUNK, WIDTH), PEER_AXES, 0, 0, tiled=...  27 us
    all_to_all x1, waiting for transfers between devices, local(): lax.all_to_all(picked.reshape(PEERS, LIST * SHARE, PAIR), PEER_AXES, 0, 0...  21.8 us
    all_to_all x1, starting transfers between devices, local(): lax.all_to_all(picked.reshape(PEERS, LIST * SHARE, PAIR), PEER_AXES, 0, 0...  9.59 us
    pallas_call x1, Pallas kernels, near_attention(): pl.pallas_call(near_kernel, grid=(KEY_HEADS,), in_specs=[pl.BlockSpec((BL...  7.54 us
    all_to_all x1, starting transfers between devices, local(): near = lax.all_to_all(near, ('y', 'x'), 0, 0, tiled=True)  3.72 us
    pallas_call x1, Pallas kernels, far_attention(): pl.pallas_call(far_kernel, in_specs=[pl.BlockSpec(memory_space=pltpu.SMEM...  3.56 us
    pallas_call x1, Pallas kernels, prep(): pl.pallas_call(prep_kernel, grid=(1,), in_specs=[pl.BlockSpec(memory_spac...  2.57 us
  transfers between devices with their start and end apart: 2, of which 1 were waited for; matrix products, arithmetic and copies ran while one was open for 1% of the time, Pallas kernels for 8%

profile of v4, /device:TPU:1, one launch (start us, length us, event | category | flops | bytes accessed | tf_op | source)
XLA Modules:
  0.0 110.9 jit_solution(777271641280103758)
XLA Ops:
  0.0 0.8 reshape.35.ids_ref
  0.8 2.6 %prep.1 = (bf16[1024,1024]{1,0:T(8,128)(2,1)}, bf16[1024,128]{1,0:T(8,128)(2,1)S(1)}) custom-call(s32[16]{0:T(128)S(1)} %reshape.35.ids_ref, bf16[64,512]{1,0:T(8,128)(2,1)} %k_ref.1, bf16[64,512]{1,0:T(8,128)(2,1)} %v_ref.1), custom_call_target="tpu_custom_call" | custom-call | tf_op jit(solution)/shard_map/prep/pallas_call | solution.py:191
  3.3 27.0 %all_to_all.21 = bf16[128,8,128]{2,1,0:T(8,128)(2,1)S(1)} all-to-all(bf16[128,8,128]{2,1,0:T(8,128)(2,1)S(1)} %bitcast.18), channel_id=1, replica_groups=mesh['zh'=4,'zl'=4,'c'=2,'y'=4,'x'=4] {'zl','c','y','x'}, dimensions={0} | all-to-all | bytes 524288 | tf_op jit(solution)/shard_map/all_to_all | solution.py:235
  30.3 3.7 %all-to-all-start.2 = ((bf16[16,64,1024]{2,1,0:T(8,128)(2,1)}), bf16[16,64,1024]{2,1,0:T(8,128)(2,1)S(1)}, u32[]{:S(2)}, u32[]{:S(2)}) async-start(bf16[16,64,1024]{2,1,0:T(8,128)(2,1)} %bitcast.9), calls=%async_computation.2 | async-start | bytes 4194304 | tf_op jit(solution)/shard_map/all_to_all | solution.py:234
  34.1 0.2 add.23
  34.3 0.1 slice.16
  34.4 0.1 copy.12
  34.5 0.1 slice.19
  34.6 0.2 copy.11
  34.8 31.3 %all_gather.3.table_ref = bf16[512,512]{1,0:T(8,128)(2,1)S(1)} all-gather(bf16[128,512]{1,0:T(8,128)(2,1)S(1)} %bitcast.23), channel_id=1, replica_groups=mesh['zh'=4,'zl'=4,'c'=2,'y'=4,'x'=4] {'zh'}, dimensions={0}, use_global_device_ids=true | all-gather | bytes 655360 | tf_op jit(solution)/shard_map/all_gather | solution.py:236
  66.0 0.2 add.20
  66.2 0.2 broadcast_add_fusion.index_ref
  66.4 1.9 %pick.1 = bf16[1024,512]{1,0:T(8,128)(2,1)} custom-call(s32[1024,2]{1,0:T(8,128)S(1)} %broadcast_add_fusion.index_ref, bf16[512,512]{1,0:T(8,128)(2,1)S(1)} %all_gather.3.table_ref), custom_call_target="tpu_custom_call" | custom-call | tf_op jit(solution)/shard_map/pick/pallas_call | solution.py:224
  68.3 0.0 all-to-all-done.2
  68.3 0.0 copy-start.2
  68.3 9.6 %all-to-all-start.1 = ((bf16[128,8,512]{2,1,0:T(8,128)(2,1)}), bf16[128,8,512]{2,1,0:T(8,128)(2,1)S(1)}, u32[]{:S(2)}, u32[]{:S(2)}) async-start(bf16[128,8,512]{2,1,0:T(8,128)(2,1)} %bitcast.7), calls=%async_computation.1 | async-start | bytes 2097152 | tf_op jit(solution)/shard_map/all_to_all | solution.py:245
  77.9 0.0 copy-done.2
  77.9 0.0 copy-start
  77.9 0.0 copy-start.1
  77.9 7.5 %near.1 = (f32[4,640,128]{2,1,0:T(8,128)S(1)}, f32[4,8,128]{2,1,0:T(8,128)S(1)}) custom-call(bf16[128,2560]{1,0:T(8,128)(2,1)} %q_ref.1, bf16[1024,1024]{1,0:T(8,128)(2,1)} %bitcast.20, bf16[1024,1024]{1,0:T(8,128)(2,1)} %bitcast.21), custom_call_target="tpu_custom_call" | custom-call | flops 67108864000 | bytes 8388608 | tf_op jit(solution)/shard_map/near/pallas_call | solution.py:80
  85.5 21.8 %all-to-all-done.1 = bf16[128,8,512]{2,1,0:T(8,128)(2,1)S(1)} async-done(((bf16[128,8,512]{2,1,0:T(8,128)(2,1)}), bf16[128,8,512]{2,1,0:T(8,128)(2,1)S(1)}, u32[]{:S(2)}, u32[]{:S(2)}) %all-to-all-start.1) | async-done | bytes 1048608 | tf_op jit(solution)/shard_map/all_to_all | solution.py:245
  107.3 0.0 copy-done
  107.3 0.0 copy-done.1
  107.3 3.6 %far.1 = bf16[128,2560]{1,0:T(8,128)(2,1)} custom-call(s32[4]{0:T(128)S(1)} %bitcast.19, bf16[128,2560]{1,0:T(8,128)(2,1)S(1)} %copy-done, bf16[1024,512]{1,0:T(8,128)(2,1)S(1)} %bitcast.17, f32[4,640,128]{2,1,0:T(8,128)S(1)} %get-tuple-element.15.mean_ref, f32[4,8,128]{2,1,0:T(8,128)S(1)} %get-tuple-element.16.log_ref), custom_call_target="tpu_custom_call" | custom-call | tf_op jit(solution)/shard_map/far/pallas_call | solution.py:144
  (4 shorter events, 0.1 us)
Async XLA Ops:
  30.3 38.0 %all-to-all-start.2 = ((bf16[16,64,1024]{2,1,0:T(8,128)(2,1)}), bf16[16,64,1024]{2,1,0:T(8,128)(2,1)S(1)}, u32[]{:S(2)}, u32[]{:S(2)}) async-start(bf16[16,64,1024]{2,1,0:T(8,128)(2,1)} %bitcast.9), calls=%async_computation.2 | async-start | bytes 4194304 | tf_op jit(solution)/shard_map/all_to_all | solution.py:234
  68.3 9.6 %copy-start.2 = (bf16[16,64,1024]{2,1,0:T(8,128)(2,1)}, bf16[16,64,1024]{2,1,0:T(8,128)(2,1)S(1)}, u32[]{:S(2)}) copy-start(bf16[16,64,1024]{2,1,0:T(8,128)(2,1)S(1)} %all-to-all-done.2) | copy-start | bytes 6291460
  68.3 39.0 %all-to-all-start.1 = ((bf16[128,8,512]{2,1,0:T(8,128)(2,1)}), bf16[128,8,512]{2,1,0:T(8,128)(2,1)S(1)}, u32[]{:S(2)}, u32[]{:S(2)}) async-start(bf16[128,8,512]{2,1,0:T(8,128)(2,1)} %bitcast.7), calls=%async_computation.1 | async-start | bytes 2097152 | tf_op jit(solution)/shard_map/all_to_all | solution.py:245
  77.9 29.4 %copy-start = (bf16[128,2560]{1,0:T(8,128)(2,1)S(1)}, bf16[128,2560]{1,0:T(8,128)(2,1)}, u32[]{:S(2)}) copy-start(bf16[128,2560]{1,0:T(8,128)(2,1)} %q_ref.1) | copy-start | bytes 1966084
  77.9 29.4 %copy-start.1 = (s32[1,4]{1,0:T(1,128)S(1)}, s32[1,4]{1,0:T(1,128)}, u32[]{:S(2)}) copy-start(s32[1,4]{1,0:T(1,128)} %param.9) | copy-start | bytes 52

commit v5 on v4

--- a/solution.py
+++ b/solution.py
@@ -13,7 +13,7 @@
 WIDTH = 128
 BLOCK = 128
 LIST = 4
-ZH, ZL, C, Y, X = 4, 4, 2, 4, 4
+ZH, ZL, C, Y, X = 8, 2, 2, 4, 4
 PEERS = ZL * C * Y * X
 PEER_AXES = ("zl", "c", "y", "x")
 KDEV = 64
@@ -21,9 +21,13 @@
 LANES = KEY_HEADS * 2 * WIDTH
 PAIR = LANES // 2
 TILES = PAIR // WIDTH
+ROWS = 2
+DATA = ROWS * TILES
+UNIT = ROWS * PAIR
 COPIES = Y * X
-CHUNK = 8
+CHUNK = 16
 SHARE = 2
+SETS = 32
 PICKED = PEERS * LIST * SHARE
 SCALE_LOG2 = math.log2(math.e) / math.sqrt(WIDTH)
 MIB = 1024 * 1024
@@ -107,13 +111,23 @@
     )
 
 
-def far_kernel(live_ref, q_ref, far_ref, mean_ref, log_ref, out_ref):
+def far_kernel(live_ref, q_ref, far_ref, mean_ref, log_ref, out_hbm, out_ref, sems):
+    copies = []
     column = lax.broadcasted_iota(jnp.int32, (1, LIST * BLOCK), 1)
     entry = (column % (LIST * SHARE)) // SHARE
     for e in range(KEY_HEADS):
-        rows = slice(e // 2 * LIST * BLOCK, (e // 2 + 1) * LIST * BLOCK)
-        k = far_ref[rows, 2 * (e % 2) * WIDTH : (2 * (e % 2) + 1) * WIDTH]
-        v = far_ref[rows, (2 * (e % 2) + 1) * WIDTH : (2 * (e % 2) + 2) * WIDTH]
+        rows = slice(e // 2 * PICKED // 2, (e // 2 + 1) * PICKED // 2)
+        tile = 2 * (e % 2)
+        k, v = (
+            jnp.concatenate(
+                [
+                    far_ref[rows, (r * TILES + t) * WIDTH : (r * TILES + t + 1) * WIDTH]
+                    for r in range(ROWS)
+                ],
+                axis=0,
+            )
+            for t in (tile, tile + 1)
+        )
         q = stack_heads(q_ref.at[:, e * GROUP * WIDTH : (e + 1) * GROUP * WIDTH])
         s = jnp.where(entry < live_ref[e], scores(q, k), -1e30)
         near_log = jnp.concatenate(
@@ -135,8 +149,12 @@
         total = back + both[:, WIDTH:]
         res = (acc / total).astype(jnp.bfloat16)
         for h in range(GROUP):
-            head = slice((e * GROUP + h) * WIDTH, (e * GROUP + h + 1) * WIDTH)
-            out_ref[:, head] = res[h * BLOCK : (h + 1) * BLOCK]
+            out_ref[e, :, h * WIDTH : (h + 1) * WIDTH] = res[h * BLOCK : (h + 1) * BLOCK]
+        heads = slice(e * GROUP * WIDTH, (e + 1) * GROUP * WIDTH)
+        copies.append(pltpu.make_async_copy(out_ref.at[e], out_hbm.at[:, heads], sems.at[e]))
+        copies[-1].start()
+    for copy in copies:
+        copy.wait()
 
 
 def far_attention(live, queries, far, mean, log):
@@ -144,8 +162,12 @@
     return pl.pallas_call(
         far_kernel,
         in_specs=[pl.BlockSpec(memory_space=pltpu.SMEM), vmem, vmem, vmem, vmem],
-        out_specs=vmem,
+        out_specs=pl.BlockSpec(memory_space=pl.ANY),
         out_shape=jax.ShapeDtypeStruct((BLOCK, KEY_HEADS * GROUP * WIDTH), jnp.bfloat16),
+        scratch_shapes=[
+            pltpu.VMEM((KEY_HEADS, BLOCK, GROUP * WIDTH), jnp.bfloat16),
+            pltpu.SemaphoreType.DMA((KEY_HEADS,)),
+        ],
         compiler_params=pltpu.CompilerParams(vmem_limit_bytes=16 * MIB),
         name="far",
     )(
@@ -157,33 +179,67 @@
     )
 
 
-def prep_kernel(ids_ref, k_ref, v_ref, near_ref, sent_ref):
+def prep_kernel(ids_ref, k_ref, v_ref, sent_ref):
     tiles = []
     for e in range(KEY_HEADS):
         tiles.append(k_ref[:, e * WIDTH : (e + 1) * WIDTH])
         tiles.append(v_ref[:, e * WIDTH : (e + 1) * WIDTH])
-    own = jnp.concatenate(tiles, axis=1)
-    for i in range(COPIES):
-        near_ref[i * KDEV : (i + 1) * KDEV] = own
-    shape = (KDEV * CHUNK, KDEV * TILES)
+    shape = (KDEV // ROWS * CHUNK, KDEV * TILES)
     row = lax.broadcasted_iota(jnp.int32, shape, 0)
     column = lax.broadcasted_iota(jnp.int32, shape, 1)
-    target = jnp.where(row % CHUNK < TILES, row % CHUNK * KDEV + row // CHUNK, -1)
+    place = row % CHUNK
+    target = place % TILES * KDEV + row // CHUNK * ROWS + place // TILES
+    target = jnp.where(place < DATA, target, -1)
     hot = jnp.where(column == target, 1.0, 0.0).astype(jnp.bfloat16)
-    shape = (KDEV * CHUNK, WIDTH)
+    shape = (KDEV // ROWS * CHUNK, WIDTH)
     lane = lax.broadcasted_iota(jnp.int32, shape, 1)
-    is_id = lax.broadcasted_iota(jnp.int32, shape, 0) % CHUNK >= TILES
+    is_id = lax.broadcasted_iota(jnp.int32, shape, 0) % CHUNK >= DATA
     ids = jnp.zeros(shape, jnp.float32)
     for i in range(KEY_HEADS * LIST):
-        ids = jnp.where(lane == i, ids_ref[i].astype(jnp.float32), ids)
+        ids = jnp.where(lane == i, ids_ref[0, i // LIST, i % LIST].astype(jnp.float32), ids)
     for j in range(2):
         moved = jnp.dot(
             hot,
             jnp.concatenate(tiles[j * TILES : (j + 1) * TILES], axis=0),
             preferred_element_type=jnp.float32,
         )
-        rows = slice(j * KDEV * CHUNK, (j + 1) * KDEV * CHUNK)
+        rows = slice(j * KDEV // ROWS * CHUNK, (j + 1) * KDEV // ROWS * CHUNK)
         sent_ref[rows] = jnp.where(is_id, ids, moved).astype(jnp.bfloat16)
+
+
+def copies_kernel(k_ref, v_ref, near_hbm, own_ref, sems):
+    tiles = []
+    for e in range(KEY_HEADS):
+        tiles.append(k_ref[:, e * WIDTH : (e + 1) * WIDTH])
+        tiles.append(v_ref[:, e * WIDTH : (e + 1) * WIDTH])
+    own_ref[...] = jnp.concatenate(tiles, axis=1)
+    moves = [
+        pltpu.make_async_copy(own_ref, near_hbm.at[i * KDEV : (i + 1) * KDEV], sems.at[i])
+        for i in range(COPIES)
+    ]
+    for move in moves:
+        move.start()
+    for move in moves:
+        move.wait()
+
+
+def copies(keys, values):
+    whole = pl.BlockSpec((KDEV, LANES // 2), lambda i: (0, 0))
+    return pl.pallas_call(
+        copies_kernel,
+        grid=(1,),
+        in_specs=[whole, whole],
+        out_specs=pl.BlockSpec(memory_space=pl.ANY),
+        out_shape=jax.ShapeDtypeStruct((COPIES * KDEV, LANES), jnp.bfloat16),
+        scratch_shapes=[
+            pltpu.VMEM((KDEV, LANES), jnp.bfloat16),
+            pltpu.SemaphoreType.DMA((COPIES,)),
+        ],
+        name="copies",
+    )(
+        pltpu.with_memory_space_constraint(keys, pltpu.HBM),
+        pltpu.with_memory_space_constraint(values, pltpu.HBM),
+    )
 
 
 def prep(ids, keys, values):
@@ -196,11 +252,8 @@
             whole((KDEV, LANES // 2)),
             whole((KDEV, LANES // 2)),
         ],
-        out_specs=[whole((COPIES * KDEV, LANES)), whole((PEERS * CHUNK, WIDTH))],
-        out_shape=[
-            jax.ShapeDtypeStruct((COPIES * KDEV, LANES), jnp.bfloat16),
-            jax.ShapeDtypeStruct((PEERS * CHUNK, WIDTH), jnp.bfloat16),
-        ],
+        out_specs=whole((PEERS * CHUNK, WIDTH)),
+        out_shape=jax.ShapeDtypeStruct((PEERS * CHUNK, WIDTH), jnp.bfloat16),
         compiler_params=pltpu.CompilerParams(vmem_limit_bytes=16 * MIB),
         name="prep",
     )(
@@ -210,44 +263,63 @@
     )
 
 
-def pick_kernel(index_ref, table_ref, out_ref):
+def pick_kernel(index_ref, *refs):
+    units, out_ref = refs[:-1], refs[-1]
     lane = lax.broadcasted_iota(jnp.int32, (PICKED, PEERS * ZH), 1)
+    table = jnp.concatenate([unit[...] for unit in units], axis=0)
     for e in range(2):
         hot = jnp.where(lane == index_ref[:, e : e + 1], 1.0, 0.0).astype(jnp.bfloat16)
-        lanes = slice(2 * WIDTH * e, 2 * WIDTH * (e + 1))
-        out_ref[:, lanes] = jnp.dot(
-            hot, table_ref[:, lanes], preferred_element_type=jnp.float32
-        ).astype(jnp.bfloat16)
-
-
-def pick(index, table):
+        for r in range(ROWS):
+            lanes = slice(r * PAIR + 2 * WIDTH * e, r * PAIR + 2 * WIDTH * (e + 1))
+            out_ref[:, lanes] = jnp.dot(
+                hot, table[:, lanes], preferred_element_type=jnp.float32
+            ).astype(jnp.bfloat16)
+
+
+def pick(index, units):
     return pl.pallas_call(
         pick_kernel,
-        out_shape=jax.ShapeDtypeStruct((PICKED, PAIR), jnp.bfloat16),
+        out_shape=pltpu.VMEM((PICKED, UNIT), jnp.bfloat16),
         compiler_params=pltpu.CompilerParams(vmem_limit_bytes=16 * MIB),
         name="pick",
-    )(index, table)
+    )(index, *units)
+
+
+def gather_sets(unit):
+    up = [(k, (k + 1) % ZH) for k in range(ZH)]
+    down = [(k, (k - 1) % ZH) for k in range(ZH)]
+    ups, downs = [unit], [unit]
+    for _ in range(ZH // 2 - 1):
+        ups.append(lax.ppermute(ups[-1], "zh", up))
+        downs.append(lax.ppermute(downs[-1], "zh", down))
+    middle = PEERS // 2
+    first = lax.ppermute(ups[-1][:middle], "zh", up)
+    second = lax.ppermute(downs[-1][middle:], "zh", down)
+    return downs + [first, second] + ups[:0:-1]
 
 
 def local(queries, keys, values, far_blocks, far_live_length):
-    near, sent = prep(far_blocks.reshape(KEY_HEADS * LIST), keys, values)
+    sent = prep(far_blocks, keys, values)
+    near = copies(keys, values)
     near = lax.all_to_all(near, ("y", "x"), 0, 0, tiled=True)
     got = lax.all_to_all(sent.reshape(PEERS, CHUNK, WIDTH), PEER_AXES, 0, 0, tiled=True)
-    table = lax.all_gather(got[:, :TILES].reshape(PEERS, PAIR), "zh", axis=0, tiled=True)
-
-    asked = got[:, TILES, : KEY_HEADS * LIST].astype(jnp.int32).reshape(PEERS, 2, 2, LIST)
+    units = gather_sets(got[:, :DATA].reshape(PEERS, UNIT))
+
+    asked = got[:, DATA, : KEY_HEADS * LIST].astype(jnp.int32).reshape(PEERS, 2, 2, LIST)
     asked = jnp.where(lax.axis_index("zl") < ZL // 2, asked[:, 0], asked[:, 1])
+    place = (asked // SETS - lax.axis_index("zh")) % ZH
     half = jnp.arange(SHARE, dtype=jnp.int32).reshape(1, 1, SHARE, 1)
-    index = asked.transpose(0, 2, 1)[:, :, None] * SHARE + half
-    picked = pick(index.reshape(PICKED, 2), table)
+    row = place * PEERS + asked % SETS * SHARE
+    index = row.transpose(0, 2, 1)[:, :, None] + half
+    picked = pick(index.reshape(PICKED, 2), units)
 
     picked, queries = lax.optimization_barrier((picked, queries))
     arrived = lax.all_to_all(
-        picked.reshape(PEERS, LIST * SHARE, PAIR), PEER_AXES, 0, 0, tiled=True
+        picked.reshape(PEERS, LIST * SHARE, UNIT), PEER_AXES, 0, 0, tiled=True
     )
     mean, log = near_attention(queries, near)
     live = far_live_length.reshape(KEY_HEADS)
-    return far_attention(live, queries, arrived.reshape(PICKED, PAIR), mean, log)
+    return far_attention(live, queries, arrived.reshape(PICKED, UNIT), mean, log)
 
 
 def solution(mesh):

time: 111 us -> 106 us (0.955)
  blocking collectives: 58.2 us -> 0 us
  starting transfers between devices: 13.3 us -> 59.9 us
  waiting for transfers between devices: 21.8 us -> 26.5 us
  Pallas kernels: 15.5 us -> 17 us
    ppermute x0 -> x8, starting transfers between devices: none -> 33.8 us  [the longest x3 16.5 us: gather_sets(): downs.append(lax.ppermute(downs[-1], 'zh', down))]
    all_gather x1 -> x0, blocking collectives: 31.3 us -> none  [local(): lax.all_gather(got[:, :TILES].reshape(PEERS, PAIR), 'zh', axis=0, tiled=T...]
    all_to_all x1 -> x0, blocking collectives: 27 us -> none  [local(): lax.all_to_all(sent.reshape(PEERS, CHUNK, WIDTH), PEER_AXES, 0, 0, tiled=...]
    all_to_all x1 -> x2, starting transfers between devices: 9.59 us -> 22.4 us  [the longest x1 11.4 us: local(): lax.all_to_all(picked.reshape(PEERS, LIST * SHARE, UNIT), PEER_AXES, 0, 0...]
    ppermute x0 -> x8, waiting for transfers between devices: none -> 10.5 us  [the longest x1 5.17 us: gather_sets(): second = lax.ppermute(downs[-1][middle:], 'zh', down)]
    all_to_all x1 -> x2, waiting for transfers between devices: 21.8 us -> 15.9 us  [the longest x1 8.96 us: local(): lax.all_to_all(picked.reshape(PEERS, LIST * SHARE, UNIT), PEER_AXES, 0, 0...]
    pallas_call x1 -> x2, Pallas kernels: 1.86 us -> 4.1 us  [the longest x1 2.37 us: copies(): pl.pallas_call(copies_kernel, grid=(1,), in_specs=[whole, whole], out_spe...]
  transfers between devices with their start and end apart: 2 -> 11, of which waited for: 1 -> 6; matrix products, arithmetic and copies ran while one was open for 1% -> 1% of each run, Pallas kernels for 8% -> 11%
where the time goes in v5:
time: 106 us; the launch traced here: 105 us
  starting transfers between devices  59.9 us (57%)
  waiting for transfers between devices  26.5 us (25%)
  Pallas kernels  17 us (16%)
  local copies, waits for them, and re-layouts  1.24 us (1%)
    ppermute x3, starting transfers between devices, gather_sets(): downs.append(lax.ppermute(downs[-1], 'zh', down))  16.5 us
    all_to_all x1, starting transfers between devices, local(): lax.all_to_all(picked.reshape(PEERS, LIST * SHARE, UNIT), PEER_AXES, 0, 0...  11.4 us
    all_to_all x1, starting transfers between devices, local(): lax.all_to_all(sent.reshape(PEERS, CHUNK, WIDTH), PEER_AXES, 0, 0, tiled=...  11 us
    ppermute x3, starting transfers between devices, gather_sets(): ups.append(lax.ppermute(ups[-1], 'zh', up))  10.6 us
    all_to_all x1, waiting for transfers between devices, local(): lax.all_to_all(picked.reshape(PEERS, LIST * SHARE, UNIT), PEER_AXES, 0, 0...  8.96 us
    pallas_call x1, Pallas kernels, near_attention(): pl.pallas_call(near_kernel, grid=(KEY_HEADS,), in_specs=[pl.BlockSpec((BL...  7.54 us
    all_to_all x1, waiting for transfers between devices, local(): lax.all_to_all(sent.reshape(PEERS, CHUNK, WIDTH), PEER_AXES, 0, 0, tiled=...  6.95 us
    ppermute x1, waiting for transfers between devices, gather_sets(): second = lax.ppermute(downs[-1][middle:], 'zh', down)  5.17 us
  transfers between devices with their start and end apart: 11, of which 6 were waited for; matrix products, arithmetic and copies ran while one was open for 1% of the time, Pallas kernels for 11%

profile of v5, /device:TPU:1, one launch (start us, length us, event | category | flops | bytes accessed | tf_op | source)
XLA Modules:
  0.0 105.0 jit_solution(353540714135247397)
XLA Ops:
  0.0 0.7 copy-done.1
  0.7 1.9 %prep.1 = bf16[1024,128]{1,0:T(8,128)(2,1)} custom-call(s32[1,4,4]{2,1,0:T(4,128)S(1)} %copy-done.1, bf16[64,512]{1,0:T(8,128)(2,1)} %k_ref.3, bf16[64,512]{1,0:T(8,128)(2,1)} %v_ref.3), custom_call_target="tpu_custom_call" | custom-call | tf_op jit(solution)/shard_map/prep/pallas_call | solution.py:247
  2.6 11.0 %all-to-all-start = ((bf16[64,16,128]{2,1,0:T(8,128)(2,1)}), bf16[64,16,128]{2,1,0:T(8,128)(2,1)S(1)}, u32[]{:S(2)}, u32[]{:S(2)}) async-start(bf16[64,16,128]{2,1,0:T(8,128)(2,1)} %bitcast.1), calls=%async_computation | async-start | bytes 524288 | tf_op jit(solution)/shard_map/all_to_all | solution.py:305
  13.6 2.4 %copies.1 = bf16[1024,1024]{1,0:T(8,128)(2,1)} custom-call(bf16[64,512]{1,0:T(8,128)(2,1)} %k_ref.3, bf16[64,512]{1,0:T(8,128)(2,1)} %v_ref.3), custom_call_target="tpu_custom_call" | custom-call | tf_op jit(solution)/shard_map/copies/pallas_call | solution.py:228
  16.0 7.0 %all-to-all-done = bf16[64,16,128]{2,1,0:T(8,128)(2,1)S(1)} async-done(((bf16[64,16,128]{2,1,0:T(8,128)(2,1)}), bf16[64,16,128]{2,1,0:T(8,128)(2,1)S(1)}, u32[]{:S(2)}, u32[]{:S(2)}) %all-to-all-start) | async-done | bytes 262176 | tf_op jit(solution)/shard_map/all_to_all | solution.py:305
  23.0 3.7 %all-to-all-start.2 = ((bf16[16,64,1024]{2,1,0:T(8,128)(2,1)}), bf16[16,64,1024]{2,1,0:T(8,128)(2,1)S(1)}, u32[]{:S(2)}, u32[]{:S(2)}) async-start(bf16[16,64,1024]{2,1,0:T(8,128)(2,1)} %bitcast.24), calls=%async_computation.2 | async-start | bytes 4194304 | tf_op jit(solution)/shard_map/all_to_all | solution.py:304
  26.7 4.2 %collective-permute-start.3 = (bf16[64,1024]{1,0:T(8,128)(2,1)S(1)}, bf16[64,1024]{1,0:T(8,128)(2,1)S(1)}, u32[]{:S(2)}, u32[]{:S(2)}) collective-permute-start(bf16[64,1024]{1,0:T(8,128)(2,1)S(1)} %bitcast.20), channel_id=1, source_target_pairs={{0,64},{64,128},{128,192},{192,256},{256,320},{320,384},{384,448},... | collective-permute-start | bytes 393224 | tf_op jit(solution)/shard_map/ppermute | solution.py:293
  30.9 7.7 %collective-permute-start = (bf16[64,1024]{1,0:T(8,128)(2,1)S(1)}, bf16[64,1024]{1,0:T(8,128)(2,1)S(1)}, u32[]{:S(2)}, u32[]{:S(2)}) collective-permute-start(bf16[64,1024]{1,0:T(8,128)(2,1)S(1)} %bitcast.21), channel_id=1, source_target_pairs={{0,448},{64,0},{128,64},{192,128},{256,192},{320,256},{384,320},{4... | collective-permute-start | bytes 393224 | tf_op jit(solution)/shard_map/ppermute | solution.py:294
  38.6 1.0 collective-permute-done.3.refs_8_
  39.7 2.2 %collective-permute-start.4 = (bf16[64,1024]{1,0:T(8,128)(2,1)S(1)}, bf16[64,1024]{1,0:T(8,128)(2,1)S(1)}, u32[]{:S(2)}, u32[]{:S(2)}) collective-permute-start(bf16[64,1024]{1,0:T(8,128)(2,1)S(1)} %collective-permute-done.3.refs_8_), channel_id=1, source_target_pairs={{0,64},{64,128},{128,192},{192,256},{256,320},{320,384},{384,448},... | collective-permute-start | bytes 393224 | tf_op jit(solution)/shard_map/ppermute | solution.py:293
  41.9 1.2 %collective-permute-done.refs_1_ = bf16[64,1024]{1,0:T(8,128)(2,1)S(1)} collective-permute-done((bf16[64,1024]{1,0:T(8,128)(2,1)S(1)}, bf16[64,1024]{1,0:T(8,128)(2,1)S(1)}, u32[]{:S(2)}, u32[]{:S(2)}) %collective-permute-start) | collective-permute-done | bytes 131104 | tf_op jit(solution)/shard_map/ppermute | solution.py:294
  43.1 5.3 %collective-permute-start.1 = (bf16[64,1024]{1,0:T(8,128)(2,1)S(1)}, bf16[64,1024]{1,0:T(8,128)(2,1)S(1)}, u32[]{:S(2)}, u32[]{:S(2)}) collective-permute-start(bf16[64,1024]{1,0:T(8,128)(2,1)S(1)} %collective-permute-done.refs_1_), channel_id=1, source_target_pairs={{0,448},{64,0},{128,64},{192,128},{256,192},{320,256},{384,320},{4... | collective-permute-start | bytes 393224 | tf_op jit(solution)/shard_map/ppermute | solution.py:294
  48.4 0.2 add.40
  48.6 0.1 copy.12
  48.7 0.0 collective-permute-done.4.refs_7_
  48.7 4.2 %collective-permute-start.5 = (bf16[64,1024]{1,0:T(8,128)(2,1)S(1)}, bf16[64,1024]{1,0:T(8,128)(2,1)S(1)}, u32[]{:S(2)}, u32[]{:S(2)}) collective-permute-start(bf16[64,1024]{1,0:T(8,128)(2,1)S(1)} %collective-permute-done.4.refs_7_), channel_id=1, source_target_pairs={{0,64},{64,128},{128,192},{192,256},{256,320},{320,384},{384,448},... | collective-permute-start | bytes 393224 | tf_op jit(solution)/shard_map/ppermute | solution.py:293
  53.0 0.0 collective-permute-done.1.refs_2_
  53.0 3.5 %collective-permute-start.2 = (bf16[64,1024]{1,0:T(8,128)(2,1)S(1)}, bf16[64,1024]{1,0:T(8,128)(2,1)S(1)}, u32[]{:S(2)}, u32[]{:S(2)}) collective-permute-start(bf16[64,1024]{1,0:T(8,128)(2,1)S(1)} %collective-permute-done.1.refs_2_), channel_id=1, source_target_pairs={{0,448},{64,0},{128,64},{192,128},{256,192},{320,256},{384,320},{4... | collective-permute-start | bytes 393224 | tf_op jit(solution)/shard_map/ppermute | solution.py:294
  56.5 0.1 copy.11
  56.7 4.8 %collective-permute-start.6 = (bf16[32,1024]{1,0:T(8,128)(2,1)S(1)}, bf16[32,1024]{1,0:T(8,128)(2,1)S(1)}, u32[]{:S(2)}, u32[]{:S(2)}) collective-permute-start(bf16[32,1024]{1,0:T(8,128)(2,1)S(1)} %slice.28), channel_id=1, source_target_pairs={{0,64},{64,128},{128,192},{192,256},{256,320},{320,384},{384,448},... | collective-permute-start | bytes 196616 | tf_op jit(solution)/shard_map/ppermute | solution.py:296
  61.5 3.1 %collective-permute-done.2.refs_3_ = bf16[64,1024]{1,0:T(8,128)(2,1)S(1)} collective-permute-done((bf16[64,1024]{1,0:T(8,128)(2,1)S(1)}, bf16[64,1024]{1,0:T(8,128)(2,1)S(1)}, u32[]{:S(2)}, u32[]{:S(2)}) %collective-permute-start.2) | collective-permute-done | bytes 131104 | tf_op jit(solution)/shard_map/ppermute | solution.py:294
  64.5 1.9 %collective-permute-start.7 = (bf16[32,1024]{1,0:T(8,128)(2,1)S(1)}, bf16[32,1024]{1,0:T(8,128)(2,1)S(1)}, u32[]{:S(2)}, u32[]{:S(2)}) collective-permute-start(bf16[32,1024]{1,0:T(8,128)(2,1)S(1)} %slice.29), channel_id=1, source_target_pairs={{0,448},{64,0},{128,64},{192,128},{256,192},{320,256},{384,320},{4... | collective-permute-start | bytes 196616 | tf_op jit(solution)/shard_map/ppermute | solution.py:297
  66.4 0.1 add.37
  66.5 0.1 broadcast_add_fusion.index_ref
  66.7 5.2 %collective-permute-done.7.refs_5_ = bf16[32,1024]{1,0:T(8,128)(2,1)S(1)} collective-permute-done((bf16[32,1024]{1,0:T(8,128)(2,1)S(1)}, bf16[32,1024]{1,0:T(8,128)(2,1)S(1)}, u32[]{:S(2)}, u32[]{:S(2)}) %collective-permute-start.7) | collective-permute-done | bytes 65568 | tf_op jit(solution)/shard_map/ppermute | solution.py:297
  71.9 1.7 %pick.1 = bf16[512,1024]{1,0:T(8,128)(2,1)} custom-call(s32[512,2]{1,0:T(8,128)S(1)} %broadcast_add_fusion.index_ref, bf16[64,1024]{1,0:T(8,128)(2,1)S(1)} %bitcast.22, bf16[64,1024]{1,0:T(8,128)(2,1)S(1)} %collective-permute-done.refs_1_, bf16[64,1024]{1,0:T(8,128)(2,1)S(1)} %collective-permute-done.1.refs_2_, ...), custom_call_target="tpu_custom_call" | custom-call | tf_op jit(solution)/shard_map/pick/pallas_call | solution.py:280
  73.6 11.4 %all-to-all-start.1 = ((bf16[64,8,1024]{2,1,0:T(8,128)(2,1)}), bf16[64,8,1024]{2,1,0:T(8,128)(2,1)S(1)}, u32[]{:S(2)}, u32[]{:S(2)}) async-start(bf16[64,8,1024]{2,1,0:T(8,128)(2,1)} %bitcast.7), calls=%async_computation.1 | async-start | bytes 2097152 | tf_op jit(solution)/shard_map/all_to_all | solution.py:317
  85.0 0.0 copy-start
  85.0 0.0 copy-start.2
  85.0 7.5 %near.1 = (f32[4,640,128]{2,1,0:T(8,128)S(1)}, f32[4,8,128]{2,1,0:T(8,128)S(1)}) custom-call(bf16[128,2560]{1,0:T(8,128)(2,1)} %q_ref.1, bf16[1024,1024]{1,0:T(8,128)(2,1)} %bitcast.25, bf16[1024,1024]{1,0:T(8,128)(2,1)} %bitcast.26), custom_call_target="tpu_custom_call" | custom-call | flops 67108864000 | bytes 8388608 | tf_op jit(solution)/shard_map/near/pallas_call | solution.py:84
  92.6 9.0 %all-to-all-done.1 = bf16[64,8,1024]{2,1,0:T(8,128)(2,1)S(1)} async-done(((bf16[64,8,1024]{2,1,0:T(8,128)(2,1)}), bf16[64,8,1024]{2,1,0:T(8,128)(2,1)S(1)}, u32[]{:S(2)}, u32[]{:S(2)}) %all-to-all-start.1) | async-done | bytes 1048608 | tf_op jit(solution)/shard_map/all_to_all | solution.py:317
  101.5 3.5 %far.1 = bf16[128,2560]{1,0:T(8,128)(2,1)} custom-call(s32[4]{0:T(128)S(1)} %bitcast.23, bf16[128,2560]{1,0:T(8,128)(2,1)S(1)} %copy-done, bf16[512,1024]{1,0:T(8,128)(2,1)S(1)} %bitcast.19, f32[4,640,128]{2,1,0:T(8,128)S(1)} %get-tuple-element.11.mean_ref, f32[4,8,128]{2,1,0:T(8,128)S(1)} %get-tuple-element.12.log_ref), custom_call_target="tpu_custom_call" | custom-call | tf_op jit(solution)/shard_map/far/pallas_call | solution.py:162
  (16 shorter events, 0.1 us)
Async XLA Ops:
  0.0 0.7 copy-start.1
  2.6 20.4 %all-to-all-start = ((bf16[64,16,128]{2,1,0:T(8,128)(2,1)}), bf16[64,16,128]{2,1,0:T(8,128)(2,1)S(1)}, u32[]{:S(2)}, u32[]{:S(2)}) async-start(bf16[64,16,128]{2,1,0:T(8,128)(2,1)} %bitcast.1), calls=%async_computation | async-start | bytes 524288 | tf_op jit(solution)/shard_map/all_to_all | solution.py:305
  23.0 50.6 %all-to-all-start.2 = ((bf16[16,64,1024]{2,1,0:T(8,128)(2,1)}), bf16[16,64,1024]{2,1,0:T(8,128)(2,1)S(1)}, u32[]{:S(2)}, u32[]{:S(2)}) async-start(bf16[16,64,1024]{2,1,0:T(8,128)(2,1)} %bitcast.24), calls=%async_computation.2 | async-start | bytes 4194304 | tf_op jit(solution)/shard_map/all_to_all | solution.py:304
  26.7 12.9 %collective-permute-start.3 = (bf16[64,1024]{1,0:T(8,128)(2,1)S(1)}, bf16[64,1024]{1,0:T(8,128)(2,1)S(1)}, u32[]{:S(2)}, u32[]{:S(2)}) collective-permute-start(bf16[64,1024]{1,0:T(8,128)(2,1)S(1)} %bitcast.20), channel_id=1, source_target_pairs={{0,64},{64,128},{128,192},{192,256},{256,320},{320,384},{384,448},... | collective-permute-start | bytes 393224 | tf_op jit(solution)/shard_map/ppermute | solution.py:293
  30.9 12.2 %collective-permute-start = (bf16[64,1024]{1,0:T(8,128)(2,1)S(1)}, bf16[64,1024]{1,0:T(8,128)(2,1)S(1)}, u32[]{:S(2)}, u32[]{:S(2)}) collective-permute-start(bf16[64,1024]{1,0:T(8,128)(2,1)S(1)} %bitcast.21), channel_id=1, source_target_pairs={{0,448},{64,0},{128,64},{192,128},{256,192},{320,256},{384,320},{4... | collective-permute-start | bytes 393224 | tf_op jit(solution)/shard_map/ppermute | solution.py:294
  39.7 9.0 %collective-permute-start.4 = (bf16[64,1024]{1,0:T(8,128)(2,1)S(1)}, bf16[64,1024]{1,0:T(8,128)(2,1)S(1)}, u32[]{:S(2)}, u32[]{:S(2)}) collective-permute-start(bf16[64,1024]{1,0:T(8,128)(2,1)S(1)} %collective-permute-done.3.refs_8_), channel_id=1, source_target_pairs={{0,64},{64,128},{128,192},{192,256},{256,320},{320,384},{384,448},... | collective-permute-start | bytes 393224 | tf_op jit(solution)/shard_map/ppermute | solution.py:293
  43.1 9.9 %collective-permute-start.1 = (bf16[64,1024]{1,0:T(8,128)(2,1)S(1)}, bf16[64,1024]{1,0:T(8,128)(2,1)S(1)}, u32[]{:S(2)}, u32[]{:S(2)}) collective-permute-start(bf16[64,1024]{1,0:T(8,128)(2,1)S(1)} %collective-permute-done.refs_1_), channel_id=1, source_target_pairs={{0,448},{64,0},{128,64},{192,128},{256,192},{320,256},{384,320},{4... | collective-permute-start | bytes 393224 | tf_op jit(solution)/shard_map/ppermute | solution.py:294
  48.7 8.0 %collective-permute-start.5 = (bf16[64,1024]{1,0:T(8,128)(2,1)S(1)}, bf16[64,1024]{1,0:T(8,128)(2,1)S(1)}, u32[]{:S(2)}, u32[]{:S(2)}) collective-permute-start(bf16[64,1024]{1,0:T(8,128)(2,1)S(1)} %collective-permute-done.4.refs_7_), channel_id=1, source_target_pairs={{0,64},{64,128},{128,192},{192,256},{256,320},{320,384},{384,448},... | collective-permute-start | bytes 393224 | tf_op jit(solution)/shard_map/ppermute | solution.py:293
  53.0 11.6 %collective-permute-start.2 = (bf16[64,1024]{1,0:T(8,128)(2,1)S(1)}, bf16[64,1024]{1,0:T(8,128)(2,1)S(1)}, u32[]{:S(2)}, u32[]{:S(2)}) collective-permute-start(bf16[64,1024]{1,0:T(8,128)(2,1)S(1)} %collective-permute-done.1.refs_2_), channel_id=1, source_target_pairs={{0,448},{64,0},{128,64},{192,128},{256,192},{320,256},{384,320},{4... | collective-permute-start | bytes 393224 | tf_op jit(solution)/shard_map/ppermute | solution.py:294
  56.7 10.0 %collective-permute-start.6 = (bf16[32,1024]{1,0:T(8,128)(2,1)S(1)}, bf16[32,1024]{1,0:T(8,128)(2,1)S(1)}, u32[]{:S(2)}, u32[]{:S(2)}) collective-permute-start(bf16[32,1024]{1,0:T(8,128)(2,1)S(1)} %slice.28), channel_id=1, source_target_pairs={{0,64},{64,128},{128,192},{192,256},{256,320},{320,384},{384,448},... | collective-permute-start | bytes 196616 | tf_op jit(solution)/shard_map/ppermute | solution.py:296
  64.5 7.3 %collective-permute-start.7 = (bf16[32,1024]{1,0:T(8,128)(2,1)S(1)}, bf16[32,1024]{1,0:T(8,128)(2,1)S(1)}, u32[]{:S(2)}, u32[]{:S(2)}) collective-permute-start(bf16[32,1024]{1,0:T(8,128)(2,1)S(1)} %slice.29), channel_id=1, source_target_pairs={{0,448},{64,0},{128,64},{192,128},{256,192},{320,256},{384,320},{4... | collective-permute-start | bytes 196616 | tf_op jit(solution)/shard_map/ppermute | solution.py:297
  73.6 11.4 %copy-start.3 = (bf16[16,64,1024]{2,1,0:T(8,128)(2,1)}, bf16[16,64,1024]{2,1,0:T(8,128)(2,1)S(1)}, u32[]{:S(2)}) copy-start(bf16[16,64,1024]{2,1,0:T(8,128)(2,1)S(1)} %all-to-all-done.2) | copy-start | bytes 6291460
  73.6 27.9 %all-to-all-start.1 = ((bf16[64,8,1024]{2,1,0:T(8,128)(2,1)}), bf16[64,8,1024]{2,1,0:T(8,128)(2,1)S(1)}, u32[]{:S(2)}, u32[]{:S(2)}) async-start(bf16[64,8,1024]{2,1,0:T(8,128)(2,1)} %bitcast.7), calls=%async_computation.1 | async-start | bytes 2097152 | tf_op jit(solution)/shard_map/all_to_all | solution.py:317
  85.0 16.5 %copy-start = (bf16[128,2560]{1,0:T(8,128)(2,1)S(1)}, bf16[128,2560]{1,0:T(8,128)(2,1)}, u32[]{:S(2)}) copy-start(bf16[128,2560]{1,0:T(8,128)(2,1)} %q_ref.1) | copy-start | bytes 1966084
  85.0 16.5 %copy-start.2 = (s32[1,4]{1,0:T(1,128)S(1)}, s32[1,4]{1,0:T(1,128)}, u32[]{:S(2)}) copy-start(s32[1,4]{1,0:T(1,128)} %param.9) | copy-start | bytes 52

commit v6 on v5

--- a/solution.py
+++ b/solution.py
@@ -248,16 +248,16 @@
         prep_kernel,
         grid=(1,),
         in_specs=[
-            pl.BlockSpec(memory_space=pltpu.SMEM),
+            pl.BlockSpec((1, KEY_HEADS, LIST), lambda i: (0, 0, 0), memory_space=pltpu.SMEM),
             whole((KDEV, LANES // 2)),
             whole((KDEV, LANES // 2)),
         ],
         out_specs=whole((PEERS * CHUNK, WIDTH)),
-        out_shape=jax.ShapeDtypeStruct((PEERS * CHUNK, WIDTH), jnp.bfloat16),
+        out_shape=pltpu.VMEM((PEERS * CHUNK, WIDTH), jnp.bfloat16),
         compiler_params=pltpu.CompilerParams(vmem_limit_bytes=16 * MIB),
         name="prep",
     )(
-        ids,
+        pltpu.with_memory_space_constraint(ids, pltpu.HBM),
         pltpu.with_memory_space_constraint(keys, pltpu.HBM),
         pltpu.with_memory_space_constraint(values, pltpu.HBM),
     )
@@ -289,13 +289,11 @@
     up = [(k, (k + 1) % ZH) for k in range(ZH)]
     down = [(k, (k - 1) % ZH) for k in range(ZH)]
     ups, downs = [unit], [unit]
-    for _ in range(ZH // 2 - 1):
+    for step in range(ZH // 2):
         ups.append(lax.ppermute(ups[-1], "zh", up))
-        downs.append(lax.ppermute(downs[-1], "zh", down))
-    middle = PEERS // 2
-    first = lax.ppermute(ups[-1][:middle], "zh", up)
-    second = lax.ppermute(downs[-1][middle:], "zh", down)
-    return downs + [first, second] + ups[:0:-1]
+        if step < ZH // 2 - 1:
+            downs.append(lax.ppermute(downs[-1], "zh", down))
+    return downs + ups[:0:-1]
 
 
 def local(queries, keys, values, far_blocks, far_live_length):

time: 106 us -> 102 us (0.962)
  waiting for transfers between devices: 26.5 us -> 21.2 us
  starting transfers between devices: 59.9 us -> 62.2 us
    ppermute x2 -> x0, starting transfers between devices: 6.66 us -> none  [the longest x1 4.75 us: gather_sets(): first = lax.ppermute(ups[-1][:middle], 'zh', up)]
    ppermute x3 -> x4, starting transfers between devices: 10.6 us -> 15.8 us  [gather_sets(): ups.append(lax.ppermute(ups[-1], 'zh', up))]
    ppermute x2 -> x0, waiting for transfers between devices: 5.17 us -> none  [the longest x1 5.17 us: gather_sets(): second = lax.ppermute(downs[-1][middle:], 'zh', down)]
    all_to_all x1, starting transfers between devices: 11.4 us -> 15.3 us  [local(): lax.all_to_all(picked.reshape(PEERS, LIST * SHARE, UNIT), PEER_AXES, 0, 0...]
  transfers between devices with their start and end apart: 11 -> 10, of which waited for: 6 -> 6; matrix products, arithmetic and copies ran while one was open for 1% -> 1% of each run, Pallas kernels for 11% -> 11%
where the time goes in v6:
time: 102 us; the launch traced here: 101 us
  starting transfers between devices  62.2 us (61%)
  waiting for transfers between devices  21.2 us (21%)
  Pallas kernels  17 us (17%)
    ppermute x3, starting transfers between devices, gather_sets(): downs.append(lax.ppermute(downs[-1], 'zh', down))  16.3 us
    ppermute x4, starting transfers between devices, gather_sets(): ups.append(lax.ppermute(ups[-1], 'zh', up))  15.8 us
    all_to_all x1, starting transfers between devices, local(): lax.all_to_all(picked.reshape(PEERS, LIST * SHARE, UNIT), PEER_AXES, 0, 0...  15.3 us
    all_to_all x1, starting transfers between devices, local(): lax.all_to_all(sent.reshape(PEERS, CHUNK, WIDTH), PEER_AXES, 0, 0, tiled=...  11 us
    all_to_all x1, waiting for transfers between devices, local(): lax.all_to_all(picked.reshape(PEERS, LIST * SHARE, UNIT), PEER_AXES, 0, 0...  8.97 us
    pallas_call x1, Pallas kernels, near_attention(): pl.pallas_call(near_kernel, grid=(KEY_HEADS,), in_specs=[pl.BlockSpec((BL...  7.54 us
    all_to_all x1, waiting for transfers between devices, local(): lax.all_to_all(sent.reshape(PEERS, CHUNK, WIDTH), PEER_AXES, 0, 0, tiled=...  6.96 us
    all_to_all x1, starting transfers between devices, local(): near = lax.all_to_all(near, ('y', 'x'), 0, 0, tiled=True)  3.72 us
  transfers between devices with their start and end apart: 10, of which 6 were waited for; matrix products, arithmetic and copies ran while one was open for 1% of the time, Pallas kernels for 11%

profile of v6, /device:TPU:1, one launch (start us, length us, event | category | flops | bytes accessed | tf_op | source)
XLA Modules:
  0.0 101.3 jit_solution(8323395079286239111)
XLA Ops:
  0.0 1.9 %prep.1 = bf16[1024,128]{1,0:T(8,128)(2,1)} custom-call(s32[1,4,4]{2,1,0:T(4,128)} %ids_ref.1, bf16[64,512]{1,0:T(8,128)(2,1)} %k_ref.3, bf16[64,512]{1,0:T(8,128)(2,1)} %v_ref.3), custom_call_target="tpu_custom_call" | custom-call | tf_op jit(solution)/shard_map/prep/pallas_call | solution.py:247
  1.9 11.0 %all-to-all-start = ((bf16[64,16,128]{2,1,0:T(8,128)(2,1)}), bf16[64,16,128]{2,1,0:T(8,128)(2,1)S(1)}, u32[]{:S(2)}, u32[]{:S(2)}) async-start(bf16[64,16,128]{2,1,0:T(8,128)(2,1)} %bitcast.1), calls=%async_computation | async-start | bytes 524288 | tf_op jit(solution)/shard_map/all_to_all | solution.py:303
  12.9 2.4 %copies.1 = bf16[1024,1024]{1,0:T(8,128)(2,1)} custom-call(bf16[64,512]{1,0:T(8,128)(2,1)} %k_ref.3, bf16[64,512]{1,0:T(8,128)(2,1)} %v_ref.3), custom_call_target="tpu_custom_call" | custom-call | tf_op jit(solution)/shard_map/copies/pallas_call | solution.py:228
  15.3 7.0 %all-to-all-done = bf16[64,16,128]{2,1,0:T(8,128)(2,1)S(1)} async-done(((bf16[64,16,128]{2,1,0:T(8,128)(2,1)}), bf16[64,16,128]{2,1,0:T(8,128)(2,1)S(1)}, u32[]{:S(2)}, u32[]{:S(2)}) %all-to-all-start) | async-done | bytes 262176 | tf_op jit(solution)/shard_map/all_to_all | solution.py:303
  22.3 3.7 %all-to-all-start.2 = ((bf16[16,64,1024]{2,1,0:T(8,128)(2,1)}), bf16[16,64,1024]{2,1,0:T(8,128)(2,1)S(1)}, u32[]{:S(2)}, u32[]{:S(2)}) async-start(bf16[16,64,1024]{2,1,0:T(8,128)(2,1)} %bitcast.24), calls=%async_computation.2 | async-start | bytes 4194304 | tf_op jit(solution)/shard_map/all_to_all | solution.py:302
  26.1 4.2 %collective-permute-start.3 = (bf16[64,1024]{1,0:T(8,128)(2,1)S(1)}, bf16[64,1024]{1,0:T(8,128)(2,1)S(1)}, u32[]{:S(2)}, u32[]{:S(2)}) collective-permute-start(bf16[64,1024]{1,0:T(8,128)(2,1)S(1)} %bitcast.20), channel_id=1, source_target_pairs={{0,64},{64,128},{128,192},{192,256},{256,320},{320,384},{384,448},... | collective-permute-start | bytes 393224 | tf_op jit(solution)/shard_map/ppermute | solution.py:293
  30.3 7.7 %collective-permute-start = (bf16[64,1024]{1,0:T(8,128)(2,1)S(1)}, bf16[64,1024]{1,0:T(8,128)(2,1)S(1)}, u32[]{:S(2)}, u32[]{:S(2)}) collective-permute-start(bf16[64,1024]{1,0:T(8,128)(2,1)S(1)} %bitcast.21), channel_id=1, source_target_pairs={{0,448},{64,0},{128,64},{192,128},{256,192},{320,256},{384,320},{4... | collective-permute-start | bytes 393224 | tf_op jit(solution)/shard_map/ppermute | solution.py:295
  37.9 1.0 %collective-permute-done.3.refs_7_ = bf16[64,1024]{1,0:T(8,128)(2,1)S(1)} collective-permute-done((bf16[64,1024]{1,0:T(8,128)(2,1)S(1)}, bf16[64,1024]{1,0:T(8,128)(2,1)S(1)}, u32[]{:S(2)}, u32[]{:S(2)}) %collective-permute-start.3) | collective-permute-done | bytes 131104 | tf_op jit(solution)/shard_map/ppermute | solution.py:293
  39.0 2.2 %collective-permute-start.4 = (bf16[64,1024]{1,0:T(8,128)(2,1)S(1)}, bf16[64,1024]{1,0:T(8,128)(2,1)S(1)}, u32[]{:S(2)}, u32[]{:S(2)}) collective-permute-start(bf16[64,1024]{1,0:T(8,128)(2,1)S(1)} %collective-permute-done.3.refs_7_), channel_id=1, source_target_pairs={{0,64},{64,128},{128,192},{192,256},{256,320},{320,384},{384,448},... | collective-permute-start | bytes 393224 | tf_op jit(solution)/shard_map/ppermute | solution.py:293
  41.2 0.2 add.40
  41.4 0.1 copy.12
  41.5 0.9 collective-permute-done.refs_1_
  42.4 5.3 %collective-permute-start.1 = (bf16[64,1024]{1,0:T(8,128)(2,1)S(1)}, bf16[64,1024]{1,0:T(8,128)(2,1)S(1)}, u32[]{:S(2)}, u32[]{:S(2)}) collective-permute-start(bf16[64,1024]{1,0:T(8,128)(2,1)S(1)} %collective-permute-done.refs_1_), channel_id=1, source_target_pairs={{0,448},{64,0},{128,64},{192,128},{256,192},{320,256},{384,320},{4... | collective-permute-start | bytes 393224 | tf_op jit(solution)/shard_map/ppermute | solution.py:295
  47.7 0.0 collective-permute-done.4.refs_6_
  47.7 4.5 %collective-permute-start.5 = (bf16[64,1024]{1,0:T(8,128)(2,1)S(1)}, bf16[64,1024]{1,0:T(8,128)(2,1)S(1)}, u32[]{:S(2)}, u32[]{:S(2)}) collective-permute-start(bf16[64,1024]{1,0:T(8,128)(2,1)S(1)} %collective-permute-done.4.refs_6_), channel_id=1, source_target_pairs={{0,64},{64,128},{128,192},{192,256},{256,320},{320,384},{384,448},... | collective-permute-start | bytes 393224 | tf_op jit(solution)/shard_map/ppermute | solution.py:293
  52.3 0.1 copy.11
  52.4 0.0 collective-permute-done.1.refs_2_
  52.5 3.4 %collective-permute-start.2 = (bf16[64,1024]{1,0:T(8,128)(2,1)S(1)}, bf16[64,1024]{1,0:T(8,128)(2,1)S(1)}, u32[]{:S(2)}, u32[]{:S(2)}) collective-permute-start(bf16[64,1024]{1,0:T(8,128)(2,1)S(1)} %collective-permute-done.1.refs_2_), channel_id=1, source_target_pairs={{0,448},{64,0},{128,64},{192,128},{256,192},{320,256},{384,320},{4... | collective-permute-start | bytes 393224 | tf_op jit(solution)/shard_map/ppermute | solution.py:295
  55.8 0.0 collective-permute-done.5.refs_5_
  55.8 4.9 %collective-permute-start.6 = (bf16[64,1024]{1,0:T(8,128)(2,1)S(1)}, bf16[64,1024]{1,0:T(8,128)(2,1)S(1)}, u32[]{:S(2)}, u32[]{:S(2)}) collective-permute-start(bf16[64,1024]{1,0:T(8,128)(2,1)S(1)} %collective-permute-done.5.refs_5_), channel_id=1, source_target_pairs={{0,64},{64,128},{128,192},{192,256},{256,320},{320,384},{384,448},... | collective-permute-start | bytes 393224 | tf_op jit(solution)/shard_map/ppermute | solution.py:293
  60.8 0.1 add.37
  60.9 0.1 broadcast_add_fusion.index_ref
  61.0 2.6 %collective-permute-done.2.refs_3_ = bf16[64,1024]{1,0:T(8,128)(2,1)S(1)} collective-permute-done((bf16[64,1024]{1,0:T(8,128)(2,1)S(1)}, bf16[64,1024]{1,0:T(8,128)(2,1)S(1)}, u32[]{:S(2)}, u32[]{:S(2)}) %collective-permute-start.2) | collective-permute-done | bytes 131104 | tf_op jit(solution)/shard_map/ppermute | solution.py:295
  63.6 0.7 collective-permute-done.6.refs_4_
  64.2 1.7 %pick.1 = bf16[512,1024]{1,0:T(8,128)(2,1)} custom-call(s32[512,2]{1,0:T(8,128)S(1)} %broadcast_add_fusion.index_ref, bf16[64,1024]{1,0:T(8,128)(2,1)S(1)} %bitcast.22, bf16[64,1024]{1,0:T(8,128)(2,1)S(1)} %collective-permute-done.refs_1_, bf16[64,1024]{1,0:T(8,128)(2,1)S(1)} %collective-permute-done.1.refs_2_, ...), custom_call_target="tpu_custom_call" | custom-call | tf_op jit(solution)/shard_map/pick/pallas_call | solution.py:280
  66.0 0.0 all-to-all-done.2
  66.0 15.3 %all-to-all-start.1 = ((bf16[64,8,1024]{2,1,0:T(8,128)(2,1)}), bf16[64,8,1024]{2,1,0:T(8,128)(2,1)S(1)}, u32[]{:S(2)}, u32[]{:S(2)}) async-start(bf16[64,8,1024]{2,1,0:T(8,128)(2,1)} %bitcast.7), calls=%async_computation.1 | async-start | bytes 2097152 | tf_op jit(solution)/shard_map/all_to_all | solution.py:315
  81.3 0.0 copy-start
  81.3 0.0 copy-start.1
  81.3 7.5 %near.1 = (f32[4,640,128]{2,1,0:T(8,128)S(1)}, f32[4,8,128]{2,1,0:T(8,128)S(1)}) custom-call(bf16[128,2560]{1,0:T(8,128)(2,1)} %q_ref.1, bf16[1024,1024]{1,0:T(8,128)(2,1)} %bitcast.25, bf16[1024,1024]{1,0:T(8,128)(2,1)} %bitcast.26), custom_call_target="tpu_custom_call" | custom-call | flops 67108864000 | bytes 8388608 | tf_op jit(solution)/shard_map/near/pallas_call | solution.py:84
  88.9 9.0 %all-to-all-done.1 = bf16[64,8,1024]{2,1,0:T(8,128)(2,1)S(1)} async-done(((bf16[64,8,1024]{2,1,0:T(8,128)(2,1)}), bf16[64,8,1024]{2,1,0:T(8,128)(2,1)S(1)}, u32[]{:S(2)}, u32[]{:S(2)}) %all-to-all-start.1) | async-done | bytes 1048608 | tf_op jit(solution)/shard_map/all_to_all | solution.py:315
  97.8 3.5 %far.1 = bf16[128,2560]{1,0:T(8,128)(2,1)} custom-call(s32[4]{0:T(128)S(1)} %bitcast.23, bf16[128,2560]{1,0:T(8,128)(2,1)S(1)} %copy-done, bf16[512,1024]{1,0:T(8,128)(2,1)S(1)} %bitcast.19, f32[4,640,128]{2,1,0:T(8,128)S(1)} %get-tuple-element.11.mean_ref, f32[4,8,128]{2,1,0:T(8,128)S(1)} %get-tuple-element.12.log_ref), custom_call_target="tpu_custom_call" | custom-call | tf_op jit(solution)/shard_map/far/pallas_call | solution.py:162
  (10 shorter events, 0.1 us)
Async XLA Ops:
  1.9 20.4 %all-to-all-start = ((bf16[64,16,128]{2,1,0:T(8,128)(2,1)}), bf16[64,16,128]{2,1,0:T(8,128)(2,1)S(1)}, u32[]{:S(2)}, u32[]{:S(2)}) async-start(bf16[64,16,128]{2,1,0:T(8,128)(2,1)} %bitcast.1), calls=%async_computation | async-start | bytes 524288 | tf_op jit(solution)/shard_map/all_to_all | solution.py:303
  22.3 43.7 %all-to-all-start.2 = ((bf16[16,64,1024]{2,1,0:T(8,128)(2,1)}), bf16[16,64,1024]{2,1,0:T(8,128)(2,1)S(1)}, u32[]{:S(2)}, u32[]{:S(2)}) async-start(bf16[16,64,1024]{2,1,0:T(8,128)(2,1)} %bitcast.24), calls=%async_computation.2 | async-start | bytes 4194304 | tf_op jit(solution)/shard_map/all_to_all | solution.py:302
  26.1 12.9 %collective-permute-start.3 = (bf16[64,1024]{1,0:T(8,128)(2,1)S(1)}, bf16[64,1024]{1,0:T(8,128)(2,1)S(1)}, u32[]{:S(2)}, u32[]{:S(2)}) collective-permute-start(bf16[64,1024]{1,0:T(8,128)(2,1)S(1)} %bitcast.20), channel_id=1, source_target_pairs={{0,64},{64,128},{128,192},{192,256},{256,320},{320,384},{384,448},... | collective-permute-start | bytes 393224 | tf_op jit(solution)/shard_map/ppermute | solution.py:293
  30.3 12.2 %collective-permute-start = (bf16[64,1024]{1,0:T(8,128)(2,1)S(1)}, bf16[64,1024]{1,0:T(8,128)(2,1)S(1)}, u32[]{:S(2)}, u32[]{:S(2)}) collective-permute-start(bf16[64,1024]{1,0:T(8,128)(2,1)S(1)} %bitcast.21), channel_id=1, source_target_pairs={{0,448},{64,0},{128,64},{192,128},{256,192},{320,256},{384,320},{4... | collective-permute-start | bytes 393224 | tf_op jit(solution)/shard_map/ppermute | solution.py:295
  39.0 8.7 %collective-permute-start.4 = (bf16[64,1024]{1,0:T(8,128)(2,1)S(1)}, bf16[64,1024]{1,0:T(8,128)(2,1)S(1)}, u32[]{:S(2)}, u32[]{:S(2)}) collective-permute-start(bf16[64,1024]{1,0:T(8,128)(2,1)S(1)} %collective-permute-done.3.refs_7_), channel_id=1, source_target_pairs={{0,64},{64,128},{128,192},{192,256},{256,320},{320,384},{384,448},... | collective-permute-start | bytes 393224 | tf_op jit(solution)/shard_map/ppermute | solution.py:293
  42.4 10.0 %collective-permute-start.1 = (bf16[64,1024]{1,0:T(8,128)(2,1)S(1)}, bf16[64,1024]{1,0:T(8,128)(2,1)S(1)}, u32[]{:S(2)}, u32[]{:S(2)}) collective-permute-start(bf16[64,1024]{1,0:T(8,128)(2,1)S(1)} %collective-permute-done.refs_1_), channel_id=1, source_target_pairs={{0,448},{64,0},{128,64},{192,128},{256,192},{320,256},{384,320},{4... | collective-permute-start | bytes 393224 | tf_op jit(solution)/shard_map/ppermute | solution.py:295
  47.7 8.1 %collective-permute-start.5 = (bf16[64,1024]{1,0:T(8,128)(2,1)S(1)}, bf16[64,1024]{1,0:T(8,128)(2,1)S(1)}, u32[]{:S(2)}, u32[]{:S(2)}) collective-permute-start(bf16[64,1024]{1,0:T(8,128)(2,1)S(1)} %collective-permute-done.4.refs_6_), channel_id=1, source_target_pairs={{0,64},{64,128},{128,192},{192,256},{256,320},{320,384},{384,448},... | collective-permute-start | bytes 393224 | tf_op jit(solution)/shard_map/ppermute | solution.py:293
  52.5 11.1 %collective-permute-start.2 = (bf16[64,1024]{1,0:T(8,128)(2,1)S(1)}, bf16[64,1024]{1,0:T(8,128)(2,1)S(1)}, u32[]{:S(2)}, u32[]{:S(2)}) collective-permute-start(bf16[64,1024]{1,0:T(8,128)(2,1)S(1)} %collective-permute-done.1.refs_2_), channel_id=1, source_target_pairs={{0,448},{64,0},{128,64},{192,128},{256,192},{320,256},{384,320},{4... | collective-permute-start | bytes 393224 | tf_op jit(solution)/shard_map/ppermute | solution.py:295
  55.8 8.4 %collective-permute-start.6 = (bf16[64,1024]{1,0:T(8,128)(2,1)S(1)}, bf16[64,1024]{1,0:T(8,128)(2,1)S(1)}, u32[]{:S(2)}, u32[]{:S(2)}) collective-permute-start(bf16[64,1024]{1,0:T(8,128)(2,1)S(1)} %collective-permute-done.5.refs_5_), channel_id=1, source_target_pairs={{0,64},{64,128},{128,192},{192,256},{256,320},{320,384},{384,448},... | collective-permute-start | bytes 393224 | tf_op jit(solution)/shard_map/ppermute | solution.py:293
  66.0 15.3 %copy-start.2 = (bf16[16,64,1024]{2,1,0:T(8,128)(2,1)}, bf16[16,64,1024]{2,1,0:T(8,128)(2,1)S(1)}, u32[]{:S(2)}) copy-start(bf16[16,64,1024]{2,1,0:T(8,128)(2,1)S(1)} %all-to-all-done.2) | copy-start | bytes 6291460
  66.0 31.9 %all-to-all-start.1 = ((bf16[64,8,1024]{2,1,0:T(8,128)(2,1)}), bf16[64,8,1024]{2,1,0:T(8,128)(2,1)S(1)}, u32[]{:S(2)}, u32[]{:S(2)}) async-start(bf16[64,8,1024]{2,1,0:T(8,128)(2,1)} %bitcast.7), calls=%async_computation.1 | async-start | bytes 2097152 | tf_op jit(solution)/shard_map/all_to_all | solution.py:315
  81.3 16.5 %copy-start = (bf16[128,2560]{1,0:T(8,128)(2,1)S(1)}, bf16[128,2560]{1,0:T(8,128)(2,1)}, u32[]{:S(2)}) copy-start(bf16[128,2560]{1,0:T(8,128)(2,1)} %q_ref.1) | copy-start | bytes 1966084
  81.3 16.5 %copy-start.1 = (s32[1,4]{1,0:T(1,128)S(1)}, s32[1,4]{1,0:T(1,128)}, u32[]{:S(2)}) copy-start(s32[1,4]{1,0:T(1,128)} %param.9) | copy-start | bytes 52

commit v7 on v6

--- a/solution.py
+++ b/solution.py
@@ -27,6 +27,7 @@
 COPIES = Y * X
 CHUNK = 16
 SHARE = 2
+LAST = ZH // 2
 SETS = 32
 PICKED = PEERS * LIST * SHARE
 SCALE_LOG2 = math.log2(math.e) / math.sqrt(WIDTH)
@@ -263,26 +264,49 @@
     )
 
 
+def chosen(index_ref, e, lane):
+    return jnp.where(lane == index_ref[:, e : e + 1], 1.0, 0.0).astype(jnp.bfloat16)
+
+
+def unit_lanes(e, r):
+    return slice(r * PAIR + 2 * WIDTH * e, r * PAIR + 2 * WIDTH * (e + 1))
+
+
 def pick_kernel(index_ref, *refs):
     units, out_ref = refs[:-1], refs[-1]
-    lane = lax.broadcasted_iota(jnp.int32, (PICKED, PEERS * ZH), 1)
+    lane = lax.broadcasted_iota(jnp.int32, (PICKED, PEERS * (ZH - 1)), 1)
+    lane = jnp.where(lane >= PEERS * LAST, lane + PEERS, lane)
     table = jnp.concatenate([unit[...] for unit in units], axis=0)
     for e in range(2):
-        hot = jnp.where(lane == index_ref[:, e : e + 1], 1.0, 0.0).astype(jnp.bfloat16)
+        hot = chosen(index_ref, e, lane)
         for r in range(ROWS):
-            lanes = slice(r * PAIR + 2 * WIDTH * e, r * PAIR + 2 * WIDTH * (e + 1))
+            lanes = unit_lanes(e, r)
             out_ref[:, lanes] = jnp.dot(
                 hot, table[:, lanes], preferred_element_type=jnp.float32
             ).astype(jnp.bfloat16)
 
 
+def pick_last_kernel(index_ref, part_ref, unit_ref, out_ref):
+    lane = lax.broadcasted_iota(jnp.int32, (PICKED, PEERS), 1) + PEERS * LAST
+    for e in range(2):
+        hot = chosen(index_ref, e, lane)
+        for r in range(ROWS):
+            lanes = unit_lanes(e, r)
+            own = jnp.dot(hot, unit_ref[:, lanes], preferred_element_type=jnp.float32)
+            out_ref[:, lanes] = part_ref[:, lanes] + own.astype(jnp.bfloat16)
+
+
 def pick(index, units):
-    return pl.pallas_call(
-        pick_kernel,
+    arguments = dict(
         out_shape=pltpu.VMEM((PICKED, UNIT), jnp.bfloat16),
         compiler_params=pltpu.CompilerParams(vmem_limit_bytes=16 * MIB),
-        name="pick",
-    )(index, *units)
+    )
+    part = pl.pallas_call(pick_kernel, name="pick", **arguments)(
+        index, *units[:LAST], *units[LAST + 1 :]
+    )
+    return pl.pallas_call(pick_last_kernel, name="pick_last", **arguments)(
+        index, part, units[LAST]
+    )
 
 
 def gather_sets(unit):

time: 102 us -> 102 us (level)
    pallas_call x1 -> x2, Pallas kernels: 1.73 us -> 2.21 us  [the longest x1 1.45 us: pick(): pl.pallas_call(pick_last_kernel, name='pick_last', **arguments)]
  transfers between devices with their start and end apart: 10 -> 10, of which waited for: 6 -> 5; matrix products, arithmetic and copies ran while one was open for 1% -> 1% of each run, Pallas kernels for 11% -> 12%
where the time goes in v7:
time: 102 us; the launch traced here: 101 us
  starting transfers between devices  62.1 us (61%)
  waiting for transfers between devices  20.5 us (20%)
  Pallas kernels  17.5 us (17%)
    ppermute x3, starting transfers between devices, gather_sets(): downs.append(lax.ppermute(downs[-1], 'zh', down))  16.3 us
    ppermute x4, starting transfers between devices, gather_sets(): ups.append(lax.ppermute(ups[-1], 'zh', up))  15.8 us
    all_to_all x1, starting transfers between devices, local(): lax.all_to_all(picked.reshape(PEERS, LIST * SHARE, UNIT), PEER_AXES, 0, 0...  15.2 us
    all_to_all x1, starting transfers between devices, local(): lax.all_to_all(sent.reshape(PEERS, CHUNK, WIDTH), PEER_AXES, 0, 0, tiled=...  11 us
    all_to_all x1, waiting for transfers between devices, local(): lax.all_to_all(picked.reshape(PEERS, LIST * SHARE, UNIT), PEER_AXES, 0, 0...  8.96 us
    pallas_call x1, Pallas kernels, near_attention(): pl.pallas_call(near_kernel, grid=(KEY_HEADS,), in_specs=[pl.BlockSpec((BL...  7.54 us
    all_to_all x1, waiting for transfers between devices, local(): lax.all_to_all(sent.reshape(PEERS, CHUNK, WIDTH), PEER_AXES, 0, 0, tiled=...  6.96 us
    all_to_all x1, starting transfers between devices, local(): near = lax.all_to_all(near, ('y', 'x'), 0, 0, tiled=True)  3.72 us
  transfers between devices with their start and end apart: 10, of which 5 were waited for; matrix products, arithmetic and copies ran while one was open for 1% of the time, Pallas kernels for 12%

profile of v7, /device:TPU:1, one launch (start us, length us, event | category | flops | bytes accessed | tf_op | source)
XLA Modules:
  0.0 101.0 jit_solution(2936361284884387877)
XLA Ops:
  0.0 1.9 %prep.1 = bf16[1024,128]{1,0:T(8,128)(2,1)} custom-call(s32[1,4,4]{2,1,0:T(4,128)} %ids_ref.1, bf16[64,512]{1,0:T(8,128)(2,1)} %k_ref.3, bf16[64,512]{1,0:T(8,128)(2,1)} %v_ref.3), custom_call_target="tpu_custom_call" | custom-call | tf_op jit(solution)/shard_map/prep/pallas_call | solution.py:248
  1.9 11.0 %all-to-all-start = ((bf16[64,16,128]{2,1,0:T(8,128)(2,1)}), bf16[64,16,128]{2,1,0:T(8,128)(2,1)S(1)}, u32[]{:S(2)}, u32[]{:S(2)}) async-start(bf16[64,16,128]{2,1,0:T(8,128)(2,1)} %bitcast.1), calls=%async_computation | async-start | bytes 524288 | tf_op jit(solution)/shard_map/all_to_all | solution.py:327
  12.9 2.4 %copies.1 = bf16[1024,1024]{1,0:T(8,128)(2,1)} custom-call(bf16[64,512]{1,0:T(8,128)(2,1)} %k_ref.3, bf16[64,512]{1,0:T(8,128)(2,1)} %v_ref.3), custom_call_target="tpu_custom_call" | custom-call | tf_op jit(solution)/shard_map/copies/pallas_call | solution.py:229
  15.3 7.0 %all-to-all-done = bf16[64,16,128]{2,1,0:T(8,128)(2,1)S(1)} async-done(((bf16[64,16,128]{2,1,0:T(8,128)(2,1)}), bf16[64,16,128]{2,1,0:T(8,128)(2,1)S(1)}, u32[]{:S(2)}, u32[]{:S(2)}) %all-to-all-start) | async-done | bytes 262176 | tf_op jit(solution)/shard_map/all_to_all | solution.py:327
  22.3 3.7 %all-to-all-start.2 = ((bf16[16,64,1024]{2,1,0:T(8,128)(2,1)}), bf16[16,64,1024]{2,1,0:T(8,128)(2,1)S(1)}, u32[]{:S(2)}, u32[]{:S(2)}) async-start(bf16[16,64,1024]{2,1,0:T(8,128)(2,1)} %bitcast.24), calls=%async_computation.2 | async-start | bytes 4194304 | tf_op jit(solution)/shard_map/all_to_all | solution.py:326
  26.1 4.2 %collective-permute-start.3 = (bf16[64,1024]{1,0:T(8,128)(2,1)S(1)}, bf16[64,1024]{1,0:T(8,128)(2,1)S(1)}, u32[]{:S(2)}, u32[]{:S(2)}) collective-permute-start(bf16[64,1024]{1,0:T(8,128)(2,1)S(1)} %bitcast.20), channel_id=1, source_target_pairs={{0,64},{64,128},{128,192},{192,256},{256,320},{320,384},{384,448},... | collective-permute-start | bytes 393224 | tf_op jit(solution)/shard_map/ppermute | solution.py:317
  30.3 7.7 %collective-permute-start = (bf16[64,1024]{1,0:T(8,128)(2,1)S(1)}, bf16[64,1024]{1,0:T(8,128)(2,1)S(1)}, u32[]{:S(2)}, u32[]{:S(2)}) collective-permute-start(bf16[64,1024]{1,0:T(8,128)(2,1)S(1)} %bitcast.21), channel_id=1, source_target_pairs={{0,448},{64,0},{128,64},{192,128},{256,192},{320,256},{384,320},{4... | collective-permute-start | bytes 393224 | tf_op jit(solution)/shard_map/ppermute | solution.py:319
  37.9 1.0 %collective-permute-done.3.refs_6_ = bf16[64,1024]{1,0:T(8,128)(2,1)S(1)} collective-permute-done((bf16[64,1024]{1,0:T(8,128)(2,1)S(1)}, bf16[64,1024]{1,0:T(8,128)(2,1)S(1)}, u32[]{:S(2)}, u32[]{:S(2)}) %collective-permute-start.3) | collective-permute-done | bytes 131104 | tf_op jit(solution)/shard_map/ppermute | solution.py:317
  39.0 2.2 %collective-permute-start.4 = (bf16[64,1024]{1,0:T(8,128)(2,1)S(1)}, bf16[64,1024]{1,0:T(8,128)(2,1)S(1)}, u32[]{:S(2)}, u32[]{:S(2)}) collective-permute-start(bf16[64,1024]{1,0:T(8,128)(2,1)S(1)} %collective-permute-done.3.refs_6_), channel_id=1, source_target_pairs={{0,64},{64,128},{128,192},{192,256},{256,320},{320,384},{384,448},... | collective-permute-start | bytes 393224 | tf_op jit(solution)/shard_map/ppermute | solution.py:317
  41.2 0.2 add.40
  41.4 0.1 copy.12
  41.5 0.9 collective-permute-done.refs_1_
  42.4 5.3 %collective-permute-start.1 = (bf16[64,1024]{1,0:T(8,128)(2,1)S(1)}, bf16[64,1024]{1,0:T(8,128)(2,1)S(1)}, u32[]{:S(2)}, u32[]{:S(2)}) collective-permute-start(bf16[64,1024]{1,0:T(8,128)(2,1)S(1)} %collective-permute-done.refs_1_), channel_id=1, source_target_pairs={{0,448},{64,0},{128,64},{192,128},{256,192},{320,256},{384,320},{4... | collective-permute-start | bytes 393224 | tf_op jit(solution)/shard_map/ppermute | solution.py:319
  47.7 0.0 collective-permute-done.4.refs_5_
  47.7 4.5 %collective-permute-start.5 = (bf16[64,1024]{1,0:T(8,128)(2,1)S(1)}, bf16[64,1024]{1,0:T(8,128)(2,1)S(1)}, u32[]{:S(2)}, u32[]{:S(2)}) collective-permute-start(bf16[64,1024]{1,0:T(8,128)(2,1)S(1)} %collective-permute-done.4.refs_5_), channel_id=1, source_target_pairs={{0,64},{64,128},{128,192},{192,256},{256,320},{320,384},{384,448},... | collective-permute-start | bytes 393224 | tf_op jit(solution)/shard_map/ppermute | solution.py:317
  52.3 0.1 copy.11
  52.4 0.0 collective-permute-done.1.refs_2_
  52.5 3.4 %collective-permute-start.2 = (bf16[64,1024]{1,0:T(8,128)(2,1)S(1)}, bf16[64,1024]{1,0:T(8,128)(2,1)S(1)}, u32[]{:S(2)}, u32[]{:S(2)}) collective-permute-start(bf16[64,1024]{1,0:T(8,128)(2,1)S(1)} %collective-permute-done.1.refs_2_), channel_id=1, source_target_pairs={{0,448},{64,0},{128,64},{192,128},{256,192},{320,256},{384,320},{4... | collective-permute-start | bytes 393224 | tf_op jit(solution)/shard_map/ppermute | solution.py:319
  55.8 0.0 collective-permute-done.5.refs_4_
  55.8 4.9 %collective-permute-start.6 = (bf16[64,1024]{1,0:T(8,128)(2,1)S(1)}, bf16[64,1024]{1,0:T(8,128)(2,1)S(1)}, u32[]{:S(2)}, u32[]{:S(2)}) collective-permute-start(bf16[64,1024]{1,0:T(8,128)(2,1)S(1)} %collective-permute-done.5.refs_4_), channel_id=1, source_target_pairs={{0,64},{64,128},{128,192},{192,256},{256,320},{320,384},{384,448},... | collective-permute-start | bytes 393224 | tf_op jit(solution)/shard_map/ppermute | solution.py:317
  60.8 0.1 add.37
  60.9 0.1 broadcast_add_fusion.index_ref
  61.0 2.6 %collective-permute-done.2.refs_3_ = bf16[64,1024]{1,0:T(8,128)(2,1)S(1)} collective-permute-done((bf16[64,1024]{1,0:T(8,128)(2,1)S(1)}, bf16[64,1024]{1,0:T(8,128)(2,1)S(1)}, u32[]{:S(2)}, u32[]{:S(2)}) %collective-permute-start.2) | collective-permute-done | bytes 131104 | tf_op jit(solution)/shard_map/ppermute | solution.py:319
  63.6 0.8 pick.1.part_ref
  64.3 1.5 %pick_last.1 = bf16[512,1024]{1,0:T(8,128)(2,1)} custom-call(s32[512,2]{1,0:T(8,128)S(1)} %broadcast_add_fusion.index_ref, bf16[512,1024]{1,0:T(8,128)(2,1)S(1)} %pick.1.part_ref, bf16[64,1024]{1,0:T(8,128)(2,1)S(1)} %collective-permute-done.6.unit_ref), custom_call_target="tpu_custom_call" | custom-call | tf_op jit(solution)/shard_map/pick_last/pallas_call | solution.py:307
  65.8 0.0 all-to-all-done.2
  65.8 15.2 %all-to-all-start.1 = ((bf16[64,8,1024]{2,1,0:T(8,128)(2,1)}), bf16[64,8,1024]{2,1,0:T(8,128)(2,1)S(1)}, u32[]{:S(2)}, u32[]{:S(2)}) async-start(bf16[64,8,1024]{2,1,0:T(8,128)(2,1)} %bitcast.7), calls=%async_computation.1 | async-start | bytes 2097152 | tf_op jit(solution)/shard_map/all_to_all | solution.py:339
  81.0 0.0 copy-start
  81.0 0.0 copy-start.1
  81.0 7.5 %near.1 = (f32[4,640,128]{2,1,0:T(8,128)S(1)}, f32[4,8,128]{2,1,0:T(8,128)S(1)}) custom-call(bf16[128,2560]{1,0:T(8,128)(2,1)} %q_ref.1, bf16[1024,1024]{1,0:T(8,128)(2,1)} %bitcast.25, bf16[1024,1024]{1,0:T(8,128)(2,1)} %bitcast.26), custom_call_target="tpu_custom_call" | custom-call | flops 67108864000 | bytes 8388608 | tf_op jit(solution)/shard_map/near/pallas_call | solution.py:85
  88.6 9.0 %all-to-all-done.1 = bf16[64,8,1024]{2,1,0:T(8,128)(2,1)S(1)} async-done(((bf16[64,8,1024]{2,1,0:T(8,128)(2,1)}), bf16[64,8,1024]{2,1,0:T(8,128)(2,1)S(1)}, u32[]{:S(2)}, u32[]{:S(2)}) %all-to-all-start.1) | async-done | bytes 1048608 | tf_op jit(solution)/shard_map/all_to_all | solution.py:339
  97.6 3.5 %far.1 = bf16[128,2560]{1,0:T(8,128)(2,1)} custom-call(s32[4]{0:T(128)S(1)} %bitcast.23, bf16[128,2560]{1,0:T(8,128)(2,1)S(1)} %copy-done, bf16[512,1024]{1,0:T(8,128)(2,1)S(1)} %bitcast.19, f32[4,640,128]{2,1,0:T(8,128)S(1)} %get-tuple-element.11.mean_ref, f32[4,8,128]{2,1,0:T(8,128)S(1)} %get-tuple-element.12.log_ref), custom_call_target="tpu_custom_call" | custom-call | tf_op jit(solution)/shard_map/far/pallas_call | solution.py:163
  (11 shorter events, 0.1 us)
Async XLA Ops:
  1.9 20.4 %all-to-all-start = ((bf16[64,16,128]{2,1,0:T(8,128)(2,1)}), bf16[64,16,128]{2,1,0:T(8,128)(2,1)S(1)}, u32[]{:S(2)}, u32[]{:S(2)}) async-start(bf16[64,16,128]{2,1,0:T(8,128)(2,1)} %bitcast.1), calls=%async_computation | async-start | bytes 524288 | tf_op jit(solution)/shard_map/all_to_all | solution.py:327
  22.3 43.5 %all-to-all-start.2 = ((bf16[16,64,1024]{2,1,0:T(8,128)(2,1)}), bf16[16,64,1024]{2,1,0:T(8,128)(2,1)S(1)}, u32[]{:S(2)}, u32[]{:S(2)}) async-start(bf16[16,64,1024]{2,1,0:T(8,128)(2,1)} %bitcast.24), calls=%async_computation.2 | async-start | bytes 4194304 | tf_op jit(solution)/shard_map/all_to_all | solution.py:326
  26.1 12.9 %collective-permute-start.3 = (bf16[64,1024]{1,0:T(8,128)(2,1)S(1)}, bf16[64,1024]{1,0:T(8,128)(2,1)S(1)}, u32[]{:S(2)}, u32[]{:S(2)}) collective-permute-start(bf16[64,1024]{1,0:T(8,128)(2,1)S(1)} %bitcast.20), channel_id=1, source_target_pairs={{0,64},{64,128},{128,192},{192,256},{256,320},{320,384},{384,448},... | collective-permute-start | bytes 393224 | tf_op jit(solution)/shard_map/ppermute | solution.py:317
  30.3 12.2 %collective-permute-start = (bf16[64,1024]{1,0:T(8,128)(2,1)S(1)}, bf16[64,1024]{1,0:T(8,128)(2,1)S(1)}, u32[]{:S(2)}, u32[]{:S(2)}) collective-permute-start(bf16[64,1024]{1,0:T(8,128)(2,1)S(1)} %bitcast.21), channel_id=1, source_target_pairs={{0,448},{64,0},{128,64},{192,128},{256,192},{320,256},{384,320},{4... | collective-permute-start | bytes 393224 | tf_op jit(solution)/shard_map/ppermute | solution.py:319
  39.0 8.7 %collective-permute-start.4 = (bf16[64,1024]{1,0:T(8,128)(2,1)S(1)}, bf16[64,1024]{1,0:T(8,128)(2,1)S(1)}, u32[]{:S(2)}, u32[]{:S(2)}) collective-permute-start(bf16[64,1024]{1,0:T(8,128)(2,1)S(1)} %collective-permute-done.3.refs_6_), channel_id=1, source_target_pairs={{0,64},{64,128},{128,192},{192,256},{256,320},{320,384},{384,448},... | collective-permute-start | bytes 393224 | tf_op jit(solution)/shard_map/ppermute | solution.py:317
  42.4 10.0 %collective-permute-start.1 = (bf16[64,1024]{1,0:T(8,128)(2,1)S(1)}, bf16[64,1024]{1,0:T(8,128)(2,1)S(1)}, u32[]{:S(2)}, u32[]{:S(2)}) collective-permute-start(bf16[64,1024]{1,0:T(8,128)(2,1)S(1)} %collective-permute-done.refs_1_), channel_id=1, source_target_pairs={{0,448},{64,0},{128,64},{192,128},{256,192},{320,256},{384,320},{4... | collective-permute-start | bytes 393224 | tf_op jit(solution)/shard_map/ppermute | solution.py:319
  47.7 8.1 %collective-permute-start.5 = (bf16[64,1024]{1,0:T(8,128)(2,1)S(1)}, bf16[64,1024]{1,0:T(8,128)(2,1)S(1)}, u32[]{:S(2)}, u32[]{:S(2)}) collective-permute-start(bf16[64,1024]{1,0:T(8,128)(2,1)S(1)} %collective-permute-done.4.refs_5_), channel_id=1, source_target_pairs={{0,64},{64,128},{128,192},{192,256},{256,320},{320,384},{384,448},... | collective-permute-start | bytes 393224 | tf_op jit(solution)/shard_map/ppermute | solution.py:317
  52.5 11.1 %collective-permute-start.2 = (bf16[64,1024]{1,0:T(8,128)(2,1)S(1)}, bf16[64,1024]{1,0:T(8,128)(2,1)S(1)}, u32[]{:S(2)}, u32[]{:S(2)}) collective-permute-start(bf16[64,1024]{1,0:T(8,128)(2,1)S(1)} %collective-permute-done.1.refs_2_), channel_id=1, source_target_pairs={{0,448},{64,0},{128,64},{192,128},{256,192},{320,256},{384,320},{4... | collective-permute-start | bytes 393224 | tf_op jit(solution)/shard_map/ppermute | solution.py:319
  55.8 8.5 %collective-permute-start.6 = (bf16[64,1024]{1,0:T(8,128)(2,1)S(1)}, bf16[64,1024]{1,0:T(8,128)(2,1)S(1)}, u32[]{:S(2)}, u32[]{:S(2)}) collective-permute-start(bf16[64,1024]{1,0:T(8,128)(2,1)S(1)} %collective-permute-done.5.refs_4_), channel_id=1, source_target_pairs={{0,64},{64,128},{128,192},{192,256},{256,320},{320,384},{384,448},... | collective-permute-start | bytes 393224 | tf_op jit(solution)/shard_map/ppermute | solution.py:317
  65.8 15.2 %copy-start.2 = (bf16[16,64,1024]{2,1,0:T(8,128)(2,1)}, bf16[16,64,1024]{2,1,0:T(8,128)(2,1)S(1)}, u32[]{:S(2)}) copy-start(bf16[16,64,1024]{2,1,0:T(8,128)(2,1)S(1)} %all-to-all-done.2) | copy-start | bytes 6291460
  65.8 31.8 %all-to-all-start.1 = ((bf16[64,8,1024]{2,1,0:T(8,128)(2,1)}), bf16[64,8,1024]{2,1,0:T(8,128)(2,1)S(1)}, u32[]{:S(2)}, u32[]{:S(2)}) async-start(bf16[64,8,1024]{2,1,0:T(8,128)(2,1)} %bitcast.7), calls=%async_computation.1 | async-start | bytes 2097152 | tf_op jit(solution)/shard_map/all_to_all | solution.py:339
  81.0 16.5 %copy-start = (bf16[128,2560]{1,0:T(8,128)(2,1)S(1)}, bf16[128,2560]{1,0:T(8,128)(2,1)}, u32[]{:S(2)}) copy-start(bf16[128,2560]{1,0:T(8,128)(2,1)} %q_ref.1) | copy-start | bytes 1966084
  81.0 16.5 %copy-start.1 = (s32[1,4]{1,0:T(1,128)S(1)}, s32[1,4]{1,0:T(1,128)}, u32[]{:S(2)}) copy-start(s32[1,4]{1,0:T(1,128)} %param.9) | copy-start | bytes 52
